TPU v7x, 256 devices: a whole 4x4x8 slice. The times are simulated.
256 devices in a mesh: dp: 2 (over y_hi), expert: 16 (over y_lo, x, core), tensor: 8 (over z).
Axes of the slice: x: 4, y: 4 (y_hi: 2, y_lo: 2; y = y_hi * 2 + y_lo), z: 8, core: 2. Of those that a mesh axis runs over, the one named last changes fastest.
Arguments:
- tokens: bfloat16 [4096, 3584], P(('dp', 'expert')), may hold values from -6 to 6
- cotangent: bfloat16 [4096, 3584], P(('dp', 'expert')), may hold values from -6 to 6
- dense_gate: bfloat16 [3584, 2432], P(('dp', 'expert'), 'tensor'), may hold values from -0.09375 to 0.09375
- dense_up: bfloat16 [3584, 2432], P(('dp', 'expert'), 'tensor'), may hold values from -0.09375 to 0.09375
- dense_down: bfloat16 [2432, 3584], P('tensor', ('dp', 'expert')), may hold values from -0.125 to 0.125
- expert_gate: bfloat16 [16, 3584, 2432], P('expert', 'dp', 'tensor'), may hold values from -0.09375 to 0.09375
- expert_up: bfloat16 [16, 3584, 2432], P('expert', 'dp', 'tensor'), may hold values from -0.09375 to 0.09375
- expert_down: bfloat16 [16, 2432, 3584], P('expert', 'tensor', 'dp'), may hold values from -0.125 to 0.125
- expert_ids: int32 [4096, 2], P(('dp', 'expert')), may hold values from 0 to 15, all different within a row; in each aligned block of 128 rows (0 to 127, 128 to 255, ...) at most 24 rows name the same one
- route_weights: float32 [4096, 2], P(('dp', 'expert')), may hold values from 0.1 to 1
Outputs:
- output: bfloat16 [4096, 3584], P(('dp', 'expert'))
- input_grad: bfloat16 [4096, 3584], P(('dp', 'expert'))
- dense_gate_grad: bfloat16 [3584, 2432], P(('dp', 'expert'), 'tensor')
- dense_up_grad: bfloat16 [3584, 2432], P(('dp', 'expert'), 'tensor')
- dense_down_grad: bfloat16 [2432, 3584], P('tensor', ('dp', 'expert'))
- expert_gate_grad: bfloat16 [16, 3584, 2432], P('expert', 'dp', 'tensor')
- expert_up_grad: bfloat16 [16, 3584, 2432], P('expert', 'dp', 'tensor')
- expert_down_grad: bfloat16 [16, 2432, 3584], P('expert', 'tensor', 'dp')
Inputs may be any that keep to these rules, and one draw needn't show every extreme that they name: `expert_ids`: the two experts of a token differ; among the 128 rows of one device no expert is named more than 24 times, and on some devices some expert is named exactly 24 times.
All inputs are finite; a program needn't handle non-finite values.
Results may differ from a plain program's by a relative error of at most 0.033.
Values may be sent and summed in bfloat16 or wider, within the bound.
A program may use at most 128 MiB of HBM per device.

v0:
```python
import jax
import jax.numpy as jnp
from jax import lax
from jax.sharding import PartitionSpec as P


def silu_pair(values):
    logistic = jax.nn.sigmoid(values)
    return (values * logistic, logistic * (1.0 + values * (1.0 - logistic)))


def product(left, right):
    return jnp.dot(left, right, preferred_element_type=jnp.float32)


def times_transposed(left, right):
    return lax.dot_general(
        left, right, (((1,), (1,)), ((), ())), preferred_element_type=jnp.float32
    )


def transposed_times(left, right):
    return lax.dot_general(
        left, right, (((0,), (0,)), ((), ())), preferred_element_type=jnp.float32
    )


def weighted_pairs(values, route_weights):
    scaled = values.astype(jnp.float32)[:, None, :] * route_weights[:, :, None]
    return scaled.astype(jnp.bfloat16).reshape(2 * values.shape[0], values.shape[1])


def shards(
    tokens,
    cotangent,
    dense_gate,
    dense_up,
    dense_down,
    expert_gate,
    expert_up,
    expert_down,
    expert_ids,
    route_weights,
):
    token_count = tokens.shape[0]
    expert_count = lax.axis_size("expert")
    capacity = max(2, 3 * token_count // expert_count)
    slot_count = expert_count * capacity
    col_width = tokens.shape[1] // lax.axis_size("tensor")
    col_start = lax.axis_index("tensor") * col_width
    flat_ids = expert_ids.reshape(-1)
    onehot = (flat_ids[:, None] == jnp.arange(expert_count, dtype=jnp.int32)[None, :]).astype(
        jnp.int32
    )
    earlier = jnp.cumsum(onehot, axis=0) - onehot
    placed = (flat_ids * capacity + jnp.sum(earlier * onehot, axis=1)).reshape(token_count, 2)
    hits = jnp.arange(slot_count, dtype=jnp.int32)[:, None, None] == placed[None, :, :]
    select_rows = jnp.any(hits, axis=2).astype(jnp.bfloat16)
    pair_select = hits.reshape(slot_count, 2 * token_count).astype(jnp.bfloat16)
    token_cols = lax.dynamic_slice_in_dim(tokens, col_start, col_width, 1)
    cot_cols = lax.dynamic_slice_in_dim(cotangent, col_start, col_width, 1)
    send_rows = product(select_rows, tokens).astype(jnp.bfloat16)
    send_cots = product(pair_select, weighted_pairs(cotangent, route_weights)).astype(jnp.bfloat16)
    arrived, cot_arrived = (
        lax.all_to_all(send_rows, "expert", split_axis=0, concat_axis=0, tiled=True),
        lax.all_to_all(send_cots, "expert", split_axis=0, concat_axis=0, tiled=True),
    )
    weight_pair = (
        lax.all_gather(expert_gate[0], "dp", axis=0, tiled=True),
        lax.all_gather(expert_up[0], "dp", axis=0, tiled=True),
    )
    weight_down = lax.all_gather(expert_down[0], "dp", axis=1, tiled=True)
    expert_pre_gate = product(arrived, weight_pair[0])
    expert_pre_up = product(arrived, weight_pair[1])
    expert_active, expert_slope = silu_pair(expert_pre_gate)
    expert_hidden = (expert_active * expert_pre_up).astype(jnp.bfloat16)
    returned = lax.psum_scatter(
        product(expert_hidden, weight_down).astype(jnp.bfloat16),
        "tensor",
        scatter_dimension=1,
        tiled=True,
    )
    came_back = lax.all_to_all(returned, "expert", split_axis=0, concat_axis=0, tiled=True)
    picked = transposed_times(pair_select, came_back).reshape(token_count, 2, col_width)
    moe_cols = jnp.sum(picked * route_weights[:, :, None], axis=1)
    dense_pair = (
        lax.all_gather(dense_gate, ("dp", "expert"), axis=0, tiled=True),
        lax.all_gather(dense_up, ("dp", "expert"), axis=0, tiled=True),
    )
    down_whole = lax.all_gather(dense_down, ("dp", "expert"), axis=1, tiled=True)
    dense_pre_gate = product(tokens, dense_pair[0])
    dense_pre_up = product(tokens, dense_pair[1])
    dense_active, dense_slope = silu_pair(dense_pre_gate)
    dense_hidden = (dense_active * dense_pre_up).astype(jnp.bfloat16)
    dense_cols = lax.psum_scatter(
        product(dense_hidden, down_whole).astype(jnp.bfloat16),
        "tensor",
        scatter_dimension=1,
        tiled=True,
    ).astype(jnp.float32)
    out_cols = (token_cols.astype(jnp.float32) + dense_cols + moe_cols).astype(jnp.bfloat16)
    output = lax.all_gather(out_cols, "tensor", axis=1, tiled=True)
    dense_grad_hidden = times_transposed(cotangent, down_whole)
    dense_grad_gate = (dense_grad_hidden * dense_pre_up * dense_slope).astype(jnp.bfloat16)
    dense_grad_up = (dense_grad_hidden * dense_active).astype(jnp.bfloat16)
    dense_in_part = times_transposed(dense_grad_gate, dense_pair[0]) + times_transposed(
        dense_grad_up, dense_pair[1]
    )
    dense_back_cols = lax.psum_scatter(
        dense_in_part.astype(jnp.bfloat16), "tensor", scatter_dimension=1, tiled=True
    ).astype(jnp.float32)
    hidden_cols = dense_gate.shape[1]
    paired = lax.psum_scatter(
        jnp.concatenate(
            [transposed_times(tokens, dense_grad_gate), transposed_times(tokens, dense_grad_up)],
            axis=1,
        ).astype(jnp.bfloat16),
        ("dp", "expert"),
        scatter_dimension=0,
        tiled=True,
    ).astype(jnp.float32)
    gate_grad = paired[:, :hidden_cols]
    up_grad = paired[:, hidden_cols:]
    down_grad = lax.psum_scatter(
        transposed_times(dense_hidden, cotangent).astype(jnp.bfloat16),
        ("dp", "expert"),
        scatter_dimension=1,
        tiled=True,
    )
    expert_grad_act = times_transposed(cot_arrived, weight_down)
    expert_grad_gate = (expert_grad_act * expert_pre_up * expert_slope).astype(jnp.bfloat16)
    expert_grad_up = (expert_grad_act * expert_active).astype(jnp.bfloat16)
    expert_in_part = times_transposed(expert_grad_gate, weight_pair[0]) + times_transposed(
        expert_grad_up, weight_pair[1]
    )
    returned_back = lax.psum_scatter(
        expert_in_part.astype(jnp.bfloat16), "tensor", scatter_dimension=1, tiled=True
    )
    back_home = lax.all_to_all(returned_back, "expert", split_axis=0, concat_axis=0, tiled=True)
    moe_back_cols = transposed_times(select_rows, back_home)
    grad_own = (cot_cols.astype(jnp.float32) + dense_back_cols + moe_back_cols).astype(jnp.bfloat16)
    input_grad = lax.all_gather(grad_own, "tensor", axis=1, tiled=True)
    grad_pair = (
        lax.psum_scatter(
            transposed_times(arrived, expert_grad_gate).astype(jnp.bfloat16),
            "dp",
            scatter_dimension=0,
            tiled=True,
        ).astype(jnp.float32),
        lax.psum_scatter(
            transposed_times(arrived, expert_grad_up).astype(jnp.bfloat16),
            "dp",
            scatter_dimension=0,
            tiled=True,
        ).astype(jnp.float32),
    )
    grad_down = lax.psum_scatter(
        transposed_times(expert_hidden, cot_arrived).astype(jnp.bfloat16),
        "dp",
        scatter_dimension=1,
        tiled=True,
    ).astype(jnp.float32)
    return (
        output,
        input_grad,
        gate_grad.astype(jnp.bfloat16),
        up_grad.astype(jnp.bfloat16),
        down_grad,
        grad_pair[0][None].astype(jnp.bfloat16),
        grad_pair[1][None].astype(jnp.bfloat16),
        grad_down[None].astype(jnp.bfloat16),
    )


def solution(mesh):
    in_specs = (
        P(("dp", "expert"), None),
        P(("dp", "expert"), None),
        P(("dp", "expert"), "tensor"),
        P(("dp", "expert"), "tensor"),
        P("tensor", ("dp", "expert")),
        P("expert", "dp", "tensor"),
        P("expert", "dp", "tensor"),
        P("expert", "tensor", "dp"),
        P(("dp", "expert"), None),
        P(("dp", "expert"), None),
    )
    out_specs = (
        P(("dp", "expert"), None),
        P(("dp", "expert"), None),
        P(("dp", "expert"), "tensor"),
        P(("dp", "expert"), "tensor"),
        P("tensor", ("dp", "expert")),
        P("expert", "dp", "tensor"),
        P("expert", "dp", "tensor"),
        P("expert", "tensor", "dp"),
    )
    return jax.shard_map(shards, mesh=mesh, in_specs=in_specs, out_specs=out_specs, check_vma=False)
```

profile of v0, /device:TPU:34, one launch (start us, length us, event | category | flops | bytes accessed | tf_op | source)
XLA Modules:
  0.0 837.8 jit_solution(12170832916250259931)
XLA Ops:
  12.2 2.4 convolution_convert_fusion.1
  14.6 6.0 all-to-all-start
  21.4 2.6 fusion.1
  24.0 34.3 %all-to-all-done = bf16[16,24,3584]{2,1,0:T(8,128)(2,1)} async-done(((bf16[16,24,3584]{2,1,0:T(8,128)(2,1)}), bf16[16,24,3584]{2,1,0:T(8,128)(2,1)}, u32[]{:S(2)}, u32[]{:S(2)}) %all-to-all-start) | async-done | bytes 2752544 | tf_op jit(solution)/shard_map/all_to_all | solution.py:65
  58.3 4.5 all-to-all-start.2
  62.8 44.5 %all-gather.13.cloned.1.call-done = bf16[1,3584,304]{1,2,0:T(8,128)(2,1)} async-done(((bf16[1,1792,304]{1,2,0:T(8,128)(2,1)}), bf16[1,3584,304]{1,2,0:T(8,128)(2,1)}) %all-gather.13.cloned.1.call-update) | async-done | bytes 2179088 | tf_op jit(solution)/shard_map/all_gather | solution.py:69
  107.3 3.7 fusion.13
  111.0 39.4 %all-gather.15.cloned.1.call-done = bf16[1,3584,304]{1,2,0:T(8,128)(2,1)} async-done(((bf16[1,1792,304]{1,2,0:T(8,128)(2,1)}), bf16[1,3584,304]{1,2,0:T(8,128)(2,1)}) %all-gather.15.cloned.1.call-update) | async-done | bytes 2179088 | tf_op jit(solution)/shard_map/all_gather | solution.py:70
  150.4 3.7 fusion.9
  154.1 38.2 %all-gather.17.cloned.1.call-done = bf16[1,304,3584]{2,1,0:T(8,128)(2,1)} async-done(((bf16[1,304,1792]{2,1,0:T(8,128)(2,1)}), bf16[1,304,3584]{2,1,0:T(8,128)(2,1)}) %all-gather.17.cloned.1.call-update) | async-done | bytes 2179088 | tf_op jit(solution)/shard_map/all_gather | solution.py:72
  192.3 4.7 multiply_convert_fusion.2
  197.0 1.9 fusion.11
  198.9 3.7 fusion
  202.9 40.4 %all-gather.19.cloned.1.call-done = bf16[32,112,304]{1,2,0:T(8,128)(2,1)} async-done(((bf16[1,112,304]{1,2,0:T(8,128)(2,1)}), bf16[32,112,304]{1,2,0:T(8,128)(2,1)}) %all-gather.19.cloned.1.call-update) | async-done | bytes 2179088 | tf_op jit(solution)/shard_map/all_gather | solution.py:87
  243.3 3.8 copy.57
  247.0 5.1 reshape.92
  252.1 42.4 %all-gather.21.cloned.1.call-done = bf16[32,112,304]{1,2,0:T(8,128)(2,1)} async-done(((bf16[1,112,304]{1,2,0:T(8,128)(2,1)}), bf16[32,112,304]{1,2,0:T(8,128)(2,1)}) %all-gather.21.cloned.1.call-update) | async-done | bytes 2179088 | tf_op jit(solution)/shard_map/all_gather | solution.py:88
  294.5 3.8 copy.58
  298.3 6.0 reshape.94
  304.3 41.5 %all-gather.23.cloned.1.call-done = bf16[32,112,304]{1,2,0:T(8,128)(2,1)} async-done(((bf16[1,112,304]{1,2,0:T(8,128)(2,1)}), bf16[32,112,304]{1,2,0:T(8,128)(2,1)}) %all-gather.23.cloned.1.call-update) | async-done | bytes 2179088 | tf_op jit(solution)/shard_map/all_gather | solution.py:90
  345.8 3.8 copy.59
  349.6 6.0 reshape.96
  359.0 1.4 multiply_convert_fusion.5
  360.3 2.1 convolution_convert_fusion.5
  362.4 4.4 copy.76
  366.9 5.2 convolution_convert_fusion
  373.8 2.2 fusion.4
  376.3 2.1 convolution_convert_fusion.8
  380.0 2.4 pad_maximum_fusion
  382.4 7.2 copy.74
  389.6 4.5 convolution_convert_fusion.3
  395.0 4.5 convolution_convert_fusion.2
  400.4 4.5 convolution_convert_fusion.4
  406.4 1.9 copy.69
  408.3 4.5 all-to-all-start.3
  413.3 69.5 %reduce-scatter.30.cloned.1.call-done = bf16[112,304]{1,0:T(8,128)(2,1)} async-done(((bf16[3584,304]{1,0:T(8,128)(2,1)}), bf16[112,304]{1,0:T(8,128)(2,1)}) %reduce-scatter.30.cloned.1.call-update) | async-done | bytes 68112
  482.8 1.6 copy.77
  484.5 44.4 %reduce-scatter.16.cloned.1.call-done = bf16[384,448]{0,1:T(8,128)(2,1)} async-done(((bf16[384,3584]{0,1:T(8,128)(2,1)}), bf16[384,448]{0,1:T(8,128)(2,1)}) %reduce-scatter.16.cloned.1.call-update) | async-done | bytes 344080 | tf_op jit(solution)/shard_map/reduce_scatter | solution.py:77
  528.8 1.9 copy.65
  530.7 5.7 all-to-all-start.1
  536.4 33.4 %reduce-scatter.18.cloned.1.call-done = bf16[128,448]{0,1:T(8,128)(2,1)} async-done(((bf16[128,3584]{0,1:T(8,128)(2,1)}), bf16[128,448]{0,1:T(8,128)(2,1)}) %reduce-scatter.18.cloned.1.call-update) | async-done | bytes 114704 | tf_op jit(solution)/shard_map/reduce_scatter | solution.py:109
  571.1 26.9 %all_gather.31 = bf16[128,3584]{0,1:T(8,128)(2,1)S(1)} all-gather(bf16[128,448]{0,1:T(8,128)(2,1)S(1)} %fusion.18), channel_id=1, replica_groups=mesh['dp'=2,'expert'=16,'tensor'=8] {'tensor'}, dimensions={1}, use_global_device_ids=true | all-gather | bytes 1032192 | tf_op jit(solution)/shard_map/all_gather | solution.py:142
  599.6 10.6 %reduce-scatter.14.cloned.1.call-done = bf16[128,448]{0,1:T(8,128)(2,1)} async-done(((bf16[128,3584]{0,1:T(8,128)(2,1)}), bf16[128,448]{0,1:T(8,128)(2,1)}) %reduce-scatter.14.cloned.1.call-update) | async-done | bytes 114704 | tf_op jit(solution)/shard_map/reduce_scatter | solution.py:95
  611.2 26.4 %all_gather.30 = bf16[128,3584]{0,1:T(8,128)(2,1)S(1)} all-gather(bf16[128,448]{0,1:T(8,128)(2,1)S(1)} %add_convert_fusion), channel_id=1, replica_groups=mesh['dp'=2,'expert'=16,'tensor'=8] {'tensor'}, dimensions={1}, use_global_device_ids=true | all-gather | bytes 1032192 | tf_op jit(solution)/shard_map/all_gather | solution.py:102
  638.8 66.8 %reduce-scatter.28.cloned.1.call-done = bf16[112,608]{1,0:T(8,128)(2,1)} async-done(((bf16[3584,608]{1,0:T(8,128)(2,1)}), bf16[112,608]{1,0:T(8,128)(2,1)}) %reduce-scatter.28.cloned.1.call-update) | async-done | bytes 136208
  708.2 39.6 %reduce-scatter.22.cloned.1.call-done = bf16[1792,304]{0,1:T(8,128)(2,1)} async-done(((bf16[3584,304]{0,1:T(8,128)(2,1)}), bf16[1792,304]{0,1:T(8,128)(2,1)}) %reduce-scatter.22.cloned.1.call-update) | async-done | bytes 1089552 | tf_op jit(solution)/shard_map/reduce_scatter | solution.py:144
  747.8 41.8 %reduce-scatter.24.cloned.1.call-done = bf16[1792,304]{0,1:T(8,128)(2,1)} async-done(((bf16[3584,304]{0,1:T(8,128)(2,1)}), bf16[1792,304]{0,1:T(8,128)(2,1)}) %reduce-scatter.24.cloned.1.call-update) | async-done | bytes 1089552 | tf_op jit(solution)/shard_map/reduce_scatter | solution.py:150
  789.6 41.7 %reduce-scatter.26.cloned.1.call-done = bf16[304,1792]{1,0:T(8,128)(2,1)} async-done(((bf16[304,3584]{1,0:T(8,128)(2,1)}), bf16[304,1792]{1,0:T(8,128)(2,1)}) %reduce-scatter.26.cloned.1.call-update) | async-done | bytes 1089552 | tf_op jit(solution)/shard_map/reduce_scatter | solution.py:157
  (101 shorter events, 24.4 us)
Async XLA Ops:
  7.2 5.0 copy-start
  7.2 3.4 copy-start.14
  7.2 100.1 %all-gather.13.cloned.1.call-start = ((), (), s32[]{:S(2)}) async-start(), calls=%async_computation.20 | async-start | bytes 3268608 | tf_op jit(solution)/shard_map/all_gather | solution.py:69
  7.9 142.5 %all-gather.15.cloned.1.call-start = ((), (), s32[]{:S(2)}) async-start(), calls=%async_computation.21 | async-start | bytes 3268608 | tf_op jit(solution)/shard_map/all_gather | solution.py:70
  8.7 183.6 %all-gather.17.cloned.1.call-start = ((), (), s32[]{:S(2)}) async-start(), calls=%async_computation.22 | async-start | bytes 3268608 | tf_op jit(solution)/shard_map/all_gather | solution.py:72
  9.4 233.9 %all-gather.19.cloned.1.call-start = ((), (), s32[]{:S(2)}) async-start(), calls=%async_computation.23 | async-start | bytes 2568192 | tf_op jit(solution)/shard_map/all_gather | solution.py:87
  10.0 284.5 %all-gather.21.cloned.1.call-start = ((), (), s32[]{:S(2)}) async-start(), calls=%async_computation.24 | async-start | bytes 2568192 | tf_op jit(solution)/shard_map/all_gather | solution.py:88
  14.6 6.6 copy-start.5
  14.6 43.7 %all-to-all-start = ((bf16[16,24,3584]{2,1,0:T(8,128)(2,1)}), bf16[16,24,3584]{2,1,0:T(8,128)(2,1)}, u32[]{:S(2)}, u32[]{:S(2)}) async-start(bf16[16,24,3584]{2,1,0:T(8,128)(2,1)} %bitcast.108), calls=%async_computation.1 | async-start | bytes 5505024 | tf_op jit(solution)/shard_map/all_to_all | solution.py:65
  20.6 0.8 copy-start.15
  20.6 325.1 %all-gather.23.cloned.1.call-start = ((), (), s32[]{:S(2)}) async-start(), calls=%async_computation.25 | async-start | bytes 2568192 | tf_op jit(solution)/shard_map/all_gather | solution.py:90
  58.3 134.0 %all-to-all-start.2 = ((bf16[16,24,3584]{2,1,0:T(8,128)(2,1)}), bf16[16,24,3584]{2,1,0:T(8,128)(2,1)}, u32[]{:S(2)}, u32[]{:S(2)}) async-start(bf16[16,24,3584]{2,1,0:T(8,128)(2,1)} %bitcast.107), calls=%async_computation.5 | async-start | bytes 5505024 | tf_op jit(solution)/shard_map/all_to_all | solution.py:66
  62.8 343.6 %reduce-scatter.20.cloned.1.call-start = ((), (), s32[]{:S(2)}) async-start(), calls=%async_computation.16 | async-start | bytes 3096576 | tf_op jit(solution)/shard_map/reduce_scatter | solution.py:136
  192.3 4.7 copy-start.8
  197.0 1.9 copy-start.9
  197.0 1.9 copy-start.7
  202.6 280.2 %reduce-scatter.30.cloned.1.call-start = ((), (), s32[]{:S(2)}) async-start(), calls=%async_computation.27 | async-start | bytes 2838528
  355.5 1.6 copy-start.1
  357.1 1.6 copy-start.3
  357.1 1.8 copy-start.6
  366.8 162.0 %reduce-scatter.16.cloned.1.call-start = ((), (), s32[]{:S(2)}) async-start(), calls=%async_computation.14 | async-start | bytes 3096576 | tf_op jit(solution)/shard_map/reduce_scatter | solution.py:77
  372.1 197.8 %reduce-scatter.18.cloned.1.call-start = ((), (), s32[]{:S(2)}) async-start(), calls=%async_computation.15 | async-start | bytes 1032192 | tf_op jit(solution)/shard_map/reduce_scatter | solution.py:109
  372.1 1.6 copy-start.2
  372.2 1.6 copy-start.11
  373.8 2.5 copy-start.4
  376.0 234.3 %reduce-scatter.14.cloned.1.call-start = ((), (), s32[]{:S(2)}) async-start(), calls=%async_computation.13 | async-start | bytes 1032192 | tf_op jit(solution)/shard_map/reduce_scatter | solution.py:95
  378.4 0.9 copy-start.12
  378.4 327.3 %reduce-scatter.28.cloned.1.call-start = ((), (), s32[]{:S(2)}) async-start(), calls=%async_computation.26 | async-start | bytes 4730880
  389.5 358.3 %reduce-scatter.22.cloned.1.call-start = ((), (), s32[]{:S(2)}) async-start(), calls=%async_computation.17 | async-start | bytes 3268608 | tf_op jit(solution)/shard_map/reduce_scatter | solution.py:144
  394.1 0.9 copy-start.10
  394.1 395.5 %reduce-scatter.24.cloned.1.call-start = ((), (), s32[]{:S(2)}) async-start(), calls=%async_computation.18 | async-start | bytes 3268608 | tf_op jit(solution)/shard_map/reduce_scatter | solution.py:150
  399.5 0.9 copy-start.13
  399.5 431.8 %reduce-scatter.26.cloned.1.call-start = ((), (), s32[]{:S(2)}) async-start(), calls=%async_computation.19 | async-start | bytes 3268608 | tf_op jit(solution)/shard_map/reduce_scatter | solution.py:157
  408.3 122.4 %all-to-all-start.3 = ((bf16[16,24,448]{2,1,0:T(8,128)(2,1)}), bf16[16,24,448]{2,1,0:T(8,128)(2,1)S(1)}, u32[]{:S(2)}, u32[]{:S(2)}) async-start(bf16[16,24,448]{2,1,0:T(8,128)(2,1)} %bitcast.16), calls=%async_computation.7 | async-start | bytes 786432 | tf_op jit(solution)/shard_map/all_to_all | solution.py:139
  530.7 68.5 %all-to-all-start.1 = ((bf16[16,24,448]{2,1,0:T(8,128)(2,1)}), bf16[16,24,448]{2,1,0:T(8,128)(2,1)S(1)}, u32[]{:S(2)}, u32[]{:S(2)}) async-start(bf16[16,24,448]{2,1,0:T(8,128)(2,1)} %bitcast.10), calls=%async_computation.3 | async-start | bytes 786432 | tf_op jit(solution)/shard_map/all_to_all | solution.py:83
Sparse Core Ops, SparseCore 0:
  9.8 97.4 all-gather.12
  109.1 41.2 all-gather.14
  152.2 40.0 all-gather.16
  194.8 48.4 all-gather.18
  245.7 48.7 all-gather.20
  297.0 48.7 all-gather.22
  348.3 43.1 reduce-scatter.19
  396.1 86.7 reduce-scatter.29
  485.6 43.2 reduce-scatter.15
  531.8 38.0 reduce-scatter.17
  573.1 37.0 reduce-scatter.13
  614.2 91.4 reduce-scatter.27
  708.8 38.9 reduce-scatter.21
  750.8 38.7 reduce-scatter.23
  792.5 38.7 reduce-scatter.25
where the time goes:
time: 841 us; the launch traced here: 838 us
  waiting for transfers between devices  632 us (75%)
  local copies, waits for them, and re-layouts  57.4 us (7%)
  matrix products  54.6 us (6%)
  blocking collectives  53.3 us (6%)
  starting transfers between devices  21.7 us (3%)
  between operations  14.2 us (2%)
    unnamed x17, waiting for transfers between devices  140 us
    all_gather x1, waiting for transfers between devices, shards(): lax.all_gather(expert_gate[0], 'dp', axis=0, tiled=True)  44.5 us
    reduce_scatter x1, waiting for transfers between devices, shards(): lax.psum_scatter(product(expert_hidden, weight_down).astype(jnp.bfloat16)...  44.4 us
    all_gather x1, waiting for transfers between devices, shards(): lax.all_gather(dense_up, ('dp', 'expert'), axis=0, tiled=True)  42.4 us
    reduce_scatter x1, waiting for transfers between devices, shards(): lax.psum_scatter(transposed_times(arrived, expert_grad_up).astype(jnp.bfl...  41.8 us
    reduce_scatter x1, waiting for transfers between devices, shards(): lax.psum_scatter(transposed_times(expert_hidden, cot_arrived).astype(jnp....  41.7 us
    all_gather x1, waiting for transfers between devices, shards(): lax.all_gather(dense_down, ('dp', 'expert'), axis=1, tiled=True)  41.5 us
    all_gather x1, waiting for transfers between devices, shards(): lax.all_gather(dense_gate, ('dp', 'expert'), axis=0, tiled=True)  40.4 us
  transfers between devices with their start and end apart: 19, of which 15 were waited for; matrix products, arithmetic and copies ran while one was open for 13% of the time, Pallas kernels for 0%

commit v1 on v0

v1 whole, which is shorter than its diff:
```python
import functools

import jax
import jax.numpy as jnp
from jax import lax
from jax.experimental import pallas as pl
from jax.experimental.pallas import tpu as pltpu
from jax.sharding import PartitionSpec as P

MESH = pl.DeviceIdType.MESH
BF = jnp.bfloat16
F32 = jnp.float32
HBM = pl.BlockSpec(memory_space=pl.ANY)
VMEM = pl.BlockSpec(memory_space=pltpu.VMEM)
DMA = pltpu.SemaphoreType.DMA
ROWS_A = pl.ds(0, 48)
ROWS_B = pl.ds(48, 64)


def silu_pair(values):
    logistic = jax.nn.sigmoid(values)
    return (values * logistic, logistic * (1.0 + values * (1.0 - logistic)))


def product(left, right):
    return jnp.dot(left, right, preferred_element_type=F32)


def times_transposed(left, right):
    return lax.dot_general(left, right, (((1,), (1,)), ((), ())), preferred_element_type=F32)


def transposed_times(left, right):
    return lax.dot_general(left, right, (((0,), (0,)), ((), ())), preferred_element_type=F32)


def place():
    dp, e, z = lax.axis_index("dp"), lax.axis_index("expert"), lax.axis_index("tensor")
    return dp * 2 + e // 8, (e // 2) % 4, e % 2, z


def device(y, x, c, z):
    return (y // 2, (y % 2) * 8 + x * 2 + c, z)


def dispatch_dest(y, x, c, z, j):
    return (y + j) % 4, (x + z // 2 + 2 * (j % 2)) % 4, (c + z) % 2


def dispatch_source(y, x, c, z, j):
    return (y + 4 - j) % 4, (x + 8 - z // 2 - 2 * (j % 2)) % 4, (c + z) % 2


def remote(src, dst, send_sem, recv_sem, dev):
    return pltpu.make_async_remote_copy(
        src_ref=src, dst_ref=dst, send_sem=send_sem, recv_sem=recv_sem, device_id=dev, device_id_type=MESH
    )


def greet(devices, conditional=()):
    barrier = pltpu.get_barrier_semaphore()
    for dev in devices:
        pl.semaphore_signal(barrier, inc=1, device_id=dev, device_id_type=MESH)
    for cond, dev in conditional:
        @pl.when(cond)
        def _():
            pl.semaphore_signal(barrier, inc=1, device_id=dev, device_id_type=MESH)
    count = jnp.int32(len(devices))
    for cond, dev in conditional:
        count = count + jnp.where(cond, jnp.int32(1), jnp.int32(0))
    pl.semaphore_wait(barrier, count)


def gather_kernel(send, w, recv, full, dsp_s, dsp_r, ring_s, ring_r, loc, d_s, d_r):
    y, x, c, z = place()
    right, left = device(y, x, c, (z + 1) % 8), device(y, x, c, (z + 7) % 8)
    xs = [device(y, (x + i) % 4, c, z) for i in (1, 2, 3)]
    ys = [device((y + i) % 4, x, c, z) for i in (1, 2, 3)]
    other = device(y, x, 1 - c, z)
    dests = [dispatch_dest(y, x, c, z, j) for j in range(4)]
    sources = [dispatch_source(y, x, c, z, j) for j in range(4)]
    greet(
        [device(*s, z) for s in sources[1:]] + xs + ys + [other, left, right],
        [(z != 0, device(*sources[0], z))],
    )

    def disp(j):
        return remote(send.at[(y + j) % 4], recv.at[z, y], dsp_s.at[j], dsp_r.at[j], device(*dests[j], z))

    here = pltpu.make_async_copy(send.at[y], recv.at[z, y], dsp_r.at[0])

    def hop(direction, t, j):
        origin = (z + 9 - t) % 8 if direction == 0 else (z + t - 1) % 8
        k = (y + 4 - j) % 4
        return remote(
            recv.at[origin, k], recv.at[origin, k],
            ring_s.at[direction, t - 1, j], ring_r.at[direction, t - 1, j], (right, left)[direction],
        )

    def members(direction, t):
        return range(4) if t < 4 else ((0, 1), (2, 3))[direction]

    @pl.when(z == 0)
    def _():
        here.start()

    @pl.when(z != 0)
    def _():
        disp(0).start()

    for j in (1, 2, 3):
        disp(j).start()

    own = pltpu.make_async_copy(w, full.at[y, x, c], loc.at[0])
    own.start()
    one_a = [remote(w.at[ROWS_A], full.at[y, x, c, ROWS_A], d_s.at[0, i], d_r.at[0, i], xs[i]) for i in range(3)]
    one_b = [remote(w.at[ROWS_B], full.at[y, x, c, ROWS_B], d_s.at[1, i], d_r.at[1, i], ys[i]) for i in range(3)]
    two_a = [
        remote(full.at[y, :, c, ROWS_A], full.at[y, :, c, ROWS_A], d_s.at[2, i], d_r.at[2, i], ys[i]) for i in range(3)
    ]
    two_b = [
        remote(full.at[:, x, c, ROWS_B], full.at[:, x, c, ROWS_B], d_s.at[3, i], d_r.at[3, i], xs[i]) for i in range(3)
    ]
    three = [remote(full.at[i, :, c], full.at[i, :, c], d_s.at[4, i], d_r.at[4, i], other) for i in range(4)]
    for copy in one_a + one_b:
        copy.start()

    for j in range(4):
        if j == 0:
            @pl.when(z == 0)
            def _():
                here.wait()

            @pl.when(z != 0)
            def _():
                disp(0).wait_recv()
        else:
            disp(j).wait_recv()
        hop(0, 1, j).start()
        hop(1, 1, j).start()
    own.wait()
    for copy in one_a + one_b:
        copy.wait_recv()
    for copy in two_a + two_b:
        copy.start()
    for t in (2, 3, 4):
        for j in range(4):
            for direction in (0, 1):
                hop(direction, t - 1, j).wait_recv()
                if j in members(direction, t):
                    hop(direction, t, j).start()
        if t == 3:
            for copy in two_a + two_b:
                copy.wait_recv()
            for copy in three:
                copy.start()
    for direction in (0, 1):
        for j in members(direction, 4):
            hop(direction, 4, j).wait_recv()
    for copy in three:
        copy.wait_recv()

    @pl.when(z != 0)
    def _():
        disp(0).wait_send()

    for j in (1, 2, 3):
        disp(j).wait_send()
    for direction in (0, 1):
        for t in (1, 2, 3, 4):
            for j in members(direction, t):
                hop(direction, t, j).wait_send()
    for copy in one_a + one_b + two_a + two_b + three:
        copy.wait_send()


def gather_call(send, w):
    return pl.pallas_call(
        gather_kernel,
        out_shape=(
            jax.ShapeDtypeStruct((8, 4, 48, send.shape[2]), BF),
            jax.ShapeDtypeStruct((4, 4, 2) + w.shape, BF),
        ),
        in_specs=[HBM, HBM],
        out_specs=(HBM, HBM),
        scratch_shapes=[DMA((4,)), DMA((4,)), DMA((2, 4, 4)), DMA((2, 4, 4)), DMA((1,)), DMA((5, 4)), DMA((5, 4))],
        compiler_params=pltpu.CompilerParams(collective_id=0, has_side_effects=True),
    )(send, w)


def swap_kernel(mine, theirs, via, s1, r1, s2, r2):
    y, x, c, z = place()
    up, down = device((y + 1) % 4, x, c, z), device((y + 3) % 4, x, c, z)
    greet([up, down])
    near = [remote(mine.at[i], via.at[i], s1.at[i], r1.at[i], (up, down)[i % 2]) for i in range(8)]
    far = [remote(via.at[i], theirs.at[i], s2.at[i], r2.at[i], (up, down)[i % 2]) for i in range(8)]
    for copy in near:
        copy.start()
    for i in range(8):
        near[i].wait_recv()
        far[i].start()
    for copy in far:
        copy.wait_recv()
    for copy in near + far:
        copy.wait_send()


def swap_call(mine):
    shape = jax.ShapeDtypeStruct(mine.shape, BF)
    return pl.pallas_call(
        swap_kernel,
        out_shape=(shape, shape),
        in_specs=[HBM],
        out_specs=(HBM, HBM),
        scratch_shapes=[DMA((8,)), DMA((8,)), DMA((8,)), DMA((8,))],
        compiler_params=pltpu.CompilerParams(collective_id=1, has_side_effects=True),
    )(mine)[0]


def add_into(dst, *others):
    total = dst[...].astype(F32)
    for other in others:
        total = total + other[...].astype(F32)
    dst[...] = total.astype(BF)


def scatter_kernel(part, dw, ret, grad, rr, cr, ra, rb, rc, rd, ring_s, ring_r, ret_s, ret_r, d_s, d_r):
    y, x, c, z = place()
    right, left = device(y, x, c, (z + 1) % 8), device(y, x, c, (z + 7) % 8)
    xi = [(x + i) % 4 for i in (1, 2, 3)]
    yi = [(y + i) % 4 for i in (1, 2, 3)]
    xs = [device(y, i, c, z) for i in xi]
    ys = [device(i, x, c, z) for i in yi]
    other = device(y, x, 1 - c, z)
    dests = [dispatch_dest(y, x, c, z, j) for j in range(4)]
    sources = [dispatch_source(y, x, c, z, j) for j in range(4)]
    greet(
        [device(*d, z) for d in dests[1:]] + xs + ys + [other, left, right],
        [(z != 0, device(*dests[0], z))],
    )

    def target(direction, u):
        return (z + 5 - u) % 8 if direction == 0 else (z + 3 + u) % 8

    def hop(direction, u, k):
        src = part.at[target(direction, u), k] if (u == 1 or (u == 2 and k not in members(direction, 1))) else rr.at[direction, u - 2, k]
        return remote(
            src, rr.at[direction, u - 1, k],
            ring_s.at[direction, u - 1, k], ring_r.at[direction, u - 1, k], (right, left)[direction],
        )

    def members(direction, u):
        return range(4) if u > 1 else ((0, 1), (2, 3))[direction]

    for direction in (0, 1):
        for k in members(direction, 1):
            hop(direction, 1, k).start()
    one = [remote(dw.at[i, :, 1 - c], cr.at[i], d_s.at[0, i], d_r.at[0, i], other) for i in range(4)]
    for copy in one:
        copy.start()
    for direction in (0, 1):
        for k in range(4):
            if k not in members(direction, 1):
                hop(direction, 2, k).start()
    for copy in one:
        copy.wait_recv()

    @pl.loop(0, 16)
    def _(i):
        add_into(cr.at[i // 4, i % 4], dw.at[i // 4, i % 4, c])

    for copy in one:
        copy.wait_send()
    two_a = [remote(cr.at[yi[i], :, ROWS_A], ra.at[i], d_s.at[1, i], d_r.at[1, i], ys[i]) for i in range(3)]
    two_b = [remote(cr.at[:, xi[i], ROWS_B], rb.at[i], d_s.at[2, i], d_r.at[2, i], xs[i]) for i in range(3)]
    for copy in two_a + two_b:
        copy.start()

    def ring_step(u):
        for k in range(4):
            for direction in (0, 1):
                if u == 2 and k not in members(direction, 1):
                    continue
                hop(direction, u - 1, k).wait_recv()
                add_into(rr.at[direction, u - 2, k], part.at[target(direction, u), k])
                hop(direction, u, k).start()

    ring_step(2)
    for copy in two_a + two_b:
        copy.wait_recv()

    @pl.loop(0, 4)
    def _(i):
        add_into(cr.at[y, i, ROWS_A], ra.at[0, i], ra.at[1, i], ra.at[2, i])
        add_into(cr.at[i, x, ROWS_B], rb.at[0, i], rb.at[1, i], rb.at[2, i])

    three_a = [remote(cr.at[y, xi[i], ROWS_A], rc.at[i], d_s.at[3, i], d_r.at[3, i], xs[i]) for i in range(3)]
    three_b = [remote(cr.at[yi[i], x, ROWS_B], rd.at[i], d_s.at[4, i], d_r.at[4, i], ys[i]) for i in range(3)]
    for copy in three_a + three_b:
        copy.start()
    ring_step(3)
    for copy in three_a + three_b:
        copy.wait_recv()
    add_into(cr.at[y, x, ROWS_A], rc.at[0], rc.at[1], rc.at[2])
    add_into(cr.at[y, x, ROWS_B], rd.at[0], rd.at[1], rd.at[2])
    grad[...] = cr[y, x]
    ring_step(4)

    def home(j):
        return remote(
            rr.at[0, 3, (y + 4 - j) % 4], ret.at[y], ret_s.at[j], ret_r.at[j], device(*sources[j], z)
        )

    here = pltpu.make_async_copy(rr.at[0, 3, y], ret.at[y], ret_r.at[0])
    for k in range(4):
        hop(0, 4, k).wait_recv()
        hop(1, 4, k).wait_recv()
        add_into(rr.at[0, 3, k], rr.at[1, 3, k], part.at[z, k])

    @pl.when(z == 0)
    def _():
        here.start()

    @pl.when(z != 0)
    def _():
        home(0).start()

    for j in (1, 2, 3):
        home(j).start()

    @pl.when(z == 0)
    def _():
        here.wait()

    @pl.when(z != 0)
    def _():
        home(0).wait()

    for j in (1, 2, 3):
        home(j).wait()
    for direction in (0, 1):
        for u in (1, 2, 3, 4):
            for k in members(direction, u):
                hop(direction, u, k).wait_send()
    for copy in two_a + two_b + three_a + three_b:
        copy.wait_send()


def scatter_call(part, dw):
    width, lanes = part.shape[3], dw.shape[4]
    return pl.pallas_call(
        scatter_kernel,
        out_shape=(
            jax.ShapeDtypeStruct((4, 48, width), BF),
            jax.ShapeDtypeStruct((112, lanes), BF),
        ),
        in_specs=[VMEM, VMEM],
        out_specs=(HBM, VMEM),
        scratch_shapes=[
            pltpu.VMEM((2, 4, 4, 48, width), BF),
            pltpu.VMEM((4, 4, 112, lanes), BF),
            pltpu.VMEM((3, 4, 48, lanes), BF),
            pltpu.VMEM((3, 4, 64, lanes), BF),
            pltpu.VMEM((3, 48, lanes), BF),
            pltpu.VMEM((3, 64, lanes), BF),
            DMA((2, 4, 4)), DMA((2, 4, 4)), DMA((4,)), DMA((4,)), DMA((5, 4)), DMA((5, 4)),
        ],
        compiler_params=pltpu.CompilerParams(
            collective_id=2, has_side_effects=True, vmem_limit_bytes=56 * 1024 * 1024
        ),
    )(part, dw)


def finish_kernel(part, tokens, cots, out, back, rr, rs_s, rs_r, ag_s, ag_r):
    y, x, c, z = place()
    right, left = device(y, x, c, (z + 1) % 8), device(y, x, c, (z + 7) % 8)
    greet([left, right])
    outs = (out, back)

    def target(direction, u):
        return (z + 5 - u) % 8 if direction == 0 else (z + 3 + u) % 8

    def hop(direction, u, q):
        src = part.at[q, target(direction, u)] if (u == 1 or (u == 2 and q != direction)) else rr.at[direction, u - 2, q]
        return remote(
            src, rr.at[direction, u - 1, q],
            rs_s.at[direction, u - 1, q], rs_r.at[direction, u - 1, q], (right, left)[direction],
        )

    def spread(direction, t, q):
        origin = (z + 9 - t) % 8 if direction == 0 else (z + t - 1) % 8
        return remote(
            outs[q].at[origin], outs[q].at[origin],
            ag_s.at[direction, t - 1, q], ag_r.at[direction, t - 1, q], (right, left)[direction],
        )

    for direction in (0, 1):
        hop(direction, 1, direction).start()
    for direction in (0, 1):
        hop(direction, 2, 1 - direction).start()
    for u in (2, 3, 4):
        for q in (0, 1):
            for direction in (0, 1):
                if u == 2 and q != direction:
                    continue
                hop(direction, u - 1, q).wait_recv()
                add_into(rr.at[direction, u - 2, q], part.at[q, target(direction, u)])
                hop(direction, u, q).start()
    for q in (0, 1):
        hop(0, 4, q).wait_recv()
        hop(1, 4, q).wait_recv()
        total = rr[0, 3, q].astype(F32) + rr[1, 3, q].astype(F32) + part[q, z].astype(F32)
        total = total + (tokens, cots)[q][z].astype(F32)
        outs[q][z] = total.astype(BF)
        for direction in (0, 1):
            spread(direction, 1, q).start()
    for t in (2, 3, 4):
        for q in (0, 1):
            for direction in (0, 1):
                spread(direction, t - 1, q).wait_recv()
                if t < 4 or q == direction:
                    spread(direction, t, q).start()
    for direction in (0, 1):
        spread(direction, 4, direction).wait_recv()
    for direction in (0, 1):
        for u in (1, 2, 3, 4):
            for q in (0, 1):
                if u > 1 or q == direction:
                    hop(direction, u, q).wait_send()
                if u < 4 or q == direction:
                    spread(direction, u, q).wait_send()


def finish_call(part, tokens, cots):
    width = part.shape[3]
    shape = jax.ShapeDtypeStruct((8, 16, width), BF)
    return pl.pallas_call(
        finish_kernel,
        out_shape=(shape, shape),
        in_specs=[VMEM, VMEM, VMEM],
        out_specs=(VMEM, VMEM),
        scratch_shapes=[
            pltpu.VMEM((2, 4, 2, 16, width), BF),
            DMA((2, 4, 2)), DMA((2, 4, 2)), DMA((2, 4, 2)), DMA((2, 4, 2)),
        ],
        compiler_params=pltpu.CompilerParams(
            collective_id=3, has_side_effects=True, vmem_limit_bytes=40 * 1024 * 1024
        ),
    )(part, tokens.reshape(8, 16, width), cots.reshape(8, 16, width))


def shards(
    tokens,
    cotangent,
    dense_gate,
    dense_up,
    dense_down,
    expert_gate,
    expert_up,
    expert_down,
    expert_ids,
    route_weights,
):
    count, width = tokens.shape
    half = width // 2
    hid = dense_gate.shape[1]
    experts, cap = 16, 24
    y, x, c, z = place()

    flat_ids = expert_ids.reshape(-1)
    onehot = (flat_ids[:, None] == jnp.arange(experts, dtype=jnp.int32)[None, :]).astype(jnp.int32)
    earlier = jnp.cumsum(onehot, axis=0) - onehot
    placed = (flat_ids * cap + jnp.sum(earlier * onehot, axis=1)).reshape(count, 2)

    y_d = jnp.arange(4, dtype=jnp.int32)
    x_d = (x + z // 2 + 2 * ((y_d + y) % 2)) % 4
    e_d = (y_d % 2) * 8 + x_d * 2 + (c + z) % 2
    slots = (e_d[:, None] * cap + jnp.arange(cap, dtype=jnp.int32)[None, :]).reshape(-1)
    hits = slots[:, None, None] == placed[None, :, :]
    select = jnp.any(hits, axis=2).astype(BF)
    weighted = jnp.sum(jnp.where(hits, route_weights[None, :, :], 0.0), axis=2)
    slot_weight = jnp.sum(weighted, axis=1)

    low, high = slice(0, 2 * cap), slice(2 * cap, 4 * cap)

    def picked(values):
        return jnp.concatenate(
            [product(select[low], values[:, :half]), product(select[high], values[:, half:])], axis=0
        )

    send_rows = picked(tokens).astype(BF).reshape(4, cap, half)
    send_cots = (picked(cotangent) * slot_weight[:, None]).astype(BF).reshape(4, cap, half)
    send = jnp.concatenate([send_rows, send_cots], axis=1)
    dense_cat = jnp.concatenate([dense_gate, dense_up, dense_down.T], axis=1)
    recv, full = gather_call(send, dense_cat)

    gate, up, down = expert_gate[0], expert_up[0], expert_down[0]
    arrived = recv[:, :, :cap].reshape(-1, half)
    cots = recv[:, :, cap:].reshape(-1, half)
    mine = jnp.concatenate(
        [product(arrived, gate), product(arrived, up), times_transposed(cots, down)], axis=1
    )
    theirs = swap_call(mine.astype(BF).reshape(8, -1, 3 * hid)).reshape(-1, 3 * hid)

    full = full.reshape(width, 3 * hid)
    both = jnp.concatenate([tokens, cotangent], axis=0)
    dense_pre = product(both, full)
    active, slope = silu_pair(dense_pre[:count, :hid])
    pre_up = dense_pre[:count, hid : 2 * hid]
    grad_act = dense_pre[count:, 2 * hid :]
    zeros = jnp.zeros((count, hid), BF)
    spread = jnp.concatenate(
        [
            jnp.concatenate([zeros, zeros, (active * pre_up).astype(BF)], axis=1),
            jnp.concatenate(
                [(grad_act * pre_up * slope).astype(BF), (grad_act * active).astype(BF), zeros], axis=1
            ),
        ],
        axis=0,
    )
    dense_part = times_transposed(spread, full)
    swapped = jnp.concatenate([cotangent, tokens], axis=0)
    dw = transposed_times(swapped, spread).astype(BF).reshape(4, 4, 2, 112, 3 * hid)

    pre = mine + theirs.astype(F32)
    active, slope = silu_pair(pre[:, :hid])
    pre_up = pre[:, hid : 2 * hid]
    grad_act = pre[:, 2 * hid :]
    hidden = (active * pre_up).astype(BF)
    grad_gate = (grad_act * pre_up * slope).astype(BF)
    grad_up = (grad_act * active).astype(BF)
    back = (times_transposed(grad_gate, gate) + times_transposed(grad_up, up)).astype(BF)
    made = product(hidden, down).astype(BF)
    part = jnp.concatenate([back.reshape(8, 4, cap, half), made.reshape(8, 4, cap, half)], axis=2)
    ret, dense_grad = scatter_call(part, dw)

    place_back = select.reshape(2, 2 * cap, count)
    place_out = weighted.astype(BF).reshape(2, 2 * cap, count)
    ret_back = ret[:, :cap].reshape(2, 2 * cap, half)
    ret_out = ret[:, cap:].reshape(2, 2 * cap, half)
    moe_out = jnp.concatenate([transposed_times(place_out[h], ret_out[h]) for h in (0, 1)], axis=1)
    moe_back = jnp.concatenate([transposed_times(place_back[h], ret_back[h]) for h in (0, 1)], axis=1)
    total = jnp.stack([dense_part[:count] + moe_out, dense_part[count:] + moe_back]).astype(BF)
    output, input_grad = finish_call(total.reshape(2, 8, 16, width), tokens, cotangent)
    return (
        output.reshape(count, width),
        input_grad.reshape(count, width),
        dense_grad[:, :hid],
        dense_grad[:, hid : 2 * hid],
        dense_grad[:, 2 * hid :].T,
        transposed_times(arrived, grad_gate).astype(BF)[None],
        transposed_times(arrived, grad_up).astype(BF)[None],
        transposed_times(hidden, cots).astype(BF)[None],
    )


def solution(mesh):
    in_specs = (
        P(("dp", "expert"), None),
        P(("dp", "expert"), None),
        P(("dp", "expert"), "tensor"),
        P(("dp", "expert"), "tensor"),
        P("tensor", ("dp", "expert")),
        P("expert", "dp", "tensor"),
        P("expert", "dp", "tensor"),
        P("expert", "tensor", "dp"),
        P(("dp", "expert"), None),
        P(("dp", "expert"), None),
    )
    out_specs = (
        P(("dp", "expert"), None),
        P(("dp", "expert"), None),
        P(("dp", "expert"), "tensor"),
        P(("dp", "expert"), "tensor"),
        P("tensor", ("dp", "expert")),
        P("expert", "dp", "tensor"),
        P("expert", "dp", "tensor"),
        P("expert", "tensor", "dp"),
    )
    return jax.shard_map(shards, mesh=mesh, in_specs=in_specs, out_specs=out_specs, check_vma=False)
```

time: 841 us -> 333 us (0.40)
  waiting for transfers between devices: 632 us -> 0 us
  Pallas kernels: 0 us -> 239 us
  blocking collectives: 53.3 us -> 0 us
  local copies, waits for them, and re-layouts: 57.4 us -> 34.4 us
  starting transfers between devices: 21.7 us -> 0 us
  matrix products: 54.6 us -> 40.5 us
  other arithmetic: 4.38 us -> 17.9 us
  between operations: 14.2 us -> 1.15 us
    all_gather x6 -> x0, waiting for transfers between devices: 246 us -> none  [the longest x1 44.5 us: shards(): lax.all_gather(expert_gate[0], 'dp', axis=0, tiled=True)]
    pallas_call x0 -> x4, Pallas kernels: none -> 239 us  [the longest x1 87.4 us: scatter_call(): pl.pallas_call(scatter_kernel, out_shape=(jax.ShapeDtypeStruct((4, 48, wi...]
    reduce_scatter x7 -> x0, waiting for transfers between devices: 212 us -> none  [the longest x1 44.4 us: shards(): lax.psum_scatter(product(expert_hidden, weight_down).astype(jnp.bfloat16)...]
    unnamed x17 -> x0, waiting for transfers between devices: 140 us -> none
    all_gather x2 -> x0, blocking collectives: 53.3 us -> none  [the longest x1 26.9 us: shards(): input_grad = lax.all_gather(grad_own, 'tensor', axis=1, tiled=True)]
    all_to_all x4 -> x0, waiting for transfers between devices: 34.3 us -> none  [the longest x1 34.3 us: shards(): lax.all_to_all(send_rows, 'expert', split_axis=0, concat_axis=0, tiled=True)]
    unnamed x45 -> x51, local copies, waits for them, and re-layouts: 39 us -> 10 us
    all_to_all x4 -> x0, starting transfers between devices: 20.7 us -> none  [the longest x1 5.99 us: shards(): lax.all_to_all(send_rows, 'expert', split_axis=0, concat_axis=0, tiled=True)]
  transfers between devices with their start and end apart: 19 -> 0, of which waited for: 15 -> 0; matrix products, arithmetic and copies ran while one was open for 13% -> 0% of each run, Pallas kernels for 0% -> 0%
where the time goes in v1:
time: 333 us
  Pallas kernels  239 us (72%)
  matrix products  40.5 us (12%)
  local copies, waits for them, and re-layouts  34.4 us (10%)
  other arithmetic  17.9 us (5%)
    pallas_call x1, Pallas kernels, scatter_call(): pl.pallas_call(scatter_kernel, out_shape=(jax.ShapeDtypeStruct((4, 48, wi...  87.4 us
    pallas_call x1, Pallas kernels, gather_call(): pl.pallas_call(gather_kernel, out_shape=(jax.ShapeDtypeStruct((8, 4, 48,...  65.7 us
    pallas_call x1, Pallas kernels, finish_call(): pl.pallas_call(finish_kernel, out_shape=(shape, shape), in_specs=[VMEM, V...  47.9 us
    pallas_call x1, Pallas kernels, swap_call(): pl.pallas_call(swap_kernel, out_shape=(shape, shape), in_specs=[HBM], out...  37.6 us
    dot_general x8, matrix products, product(): return jnp.dot(left, right, preferred_element_type=F32)  18.9 us
    dot_general x8, matrix products, transposed_times(): lax.dot_general(left, right, (((0,), (0,)), ((), ())), preferred_element_...  11.9 us
    convert_element_type x1, local copies, waits for them, and re-layouts, shards(): transposed_times(swapped, spread).astype(BF).reshape(4, 4, 2, 112, 3 * hid)  10.2 us
    unnamed x51, local copies, waits for them, and re-layouts  10 us

profile of v1, /device:TPU:34, one launch (start us, length us, event | category | flops | bytes accessed | tf_op | source)
XLA Modules:
  0.0 332.6 jit_solution(7793504152869201054)
XLA Ops:
  0.9 0.9 copy.65
  2.1 0.6 reduce-window.6
  3.2 0.7 multiply_add_fusion
  4.0 0.9 select_reduce_fusion
  5.0 1.0 copy.70
  6.0 1.0 copy.71
  7.0 1.0 copy.69
  8.0 0.8 pad_maximum_fusion.6.w
  8.8 1.2 convolution_convert_fusion.5
  10.0 1.2 convolution_convert_fusion.6
  11.9 0.9 pad_maximum_fusion.4.send
  12.8 65.7 %shard_map.161 = (bf16[8,4,48,1792]{3,2,1,0:T(8,128)(2,1)}, bf16[4,4,2,112,912]{4,3,2,1,0:T(8,128)(2,1)}) custom-call(bf16[4,48,1792]{2,1,0:T(8,128)(2,1)} %pad_maximum_fusion.4.send, bf16[112,912]{1,0:T(8,128)(2,1)} %pad_maximum_fusion.6.w), custom_call_target="tpu_custom_call" | custom-call | tf_op jit(solution)/shard_map/pallas_call | solution.py:178
  78.5 6.1 %fusion.5 = f32[256,912]{0,1:T(8,128)S(1)} fusion(bf16[3584,912]{1,0:T(8,128)(2,1)} %bitcast.118, bf16[128,3584]{1,0:T(8,128)(2,1)S(1)} %copy-done.2, bf16[128,3584]{1,0:T(8,128)(2,1)S(1)} %copy-done.3), kind=kOutput, calls=%fused_computation.17 | convolution fusion | flops 1677197312 | bytes 9306112 | tf_op jit(solution)/shard_map/dot_general | solution.py:26
  84.8 4.0 %fusion.33 = f32[256,3584]{1,0:T(8,128)} fusion(bf16[3584,912]{1,0:T(8,128)(2,1)S(1)} %bitcast.119, bf16[128,304]{0,1:T(8,128)(2,1)S(1)} %get-tuple-element.64, bf16[128,304]{0,1:T(8,128)(2,1)S(1)} %broadcast_in_dim.31, bf16[128,304]{0,1:T(8,128)(2,1)S(1)} %get-tuple-element.65, bf16[128,304]{0,1:T(8,128)(2,1)S(1)} %get-tuple-element.63), kind=kOutput, calls=%fused_computation.64 | convolution fusion | flops 1675862016 | bytes 10518528 | tf_op jit(solution)/shard_map/dot_general | solution.py:30
  88.9 2.0 fusion.65
  90.9 2.2 fusion.67
  93.1 1.3 copy.74
  94.4 4.2 %fusion.68 = (bf16[768,304]{0,1:T(8,128)(2,1)}, f32[768,304]{0,1:T(8,128)}) fusion(bf16[768,1792]{1,0:T(8,128)(2,1)} %bitcast.101, bf16[1,1792,304]{1,2,0:T(8,128)(2,1)} %param.16), kind=kOutput, calls=%fused_computation.114 | convolution fusion | flops 836997120 | bytes 5242880 | tf_op jit(solution)/shard_map/dot_general | solution.py:26
  98.6 2.1 copy.73
  100.7 4.2 %fusion.69 = (bf16[768,304]{0,1:T(8,128)(2,1)}, f32[768,304]{0,1:T(8,128)}) fusion(bf16[768,1792]{1,0:T(8,128)(2,1)} %bitcast.102, bf16[1,1792,304]{1,2,0:T(8,128)(2,1)} %param.15), kind=kOutput, calls=%fused_computation.115 | convolution fusion | flops 836997120 | bytes 5242880 | tf_op jit(solution)/shard_map/dot_general | solution.py:26
  104.9 2.1 copy.72
  106.9 3.2 pad_maximum_fusion.2.mine
  110.1 37.6 %shard_map.162 = (bf16[8,96,912]{2,1,0:T(8,128)(2,1)}, bf16[8,96,912]{2,1,0:T(8,128)(2,1)}) custom-call(bf16[8,96,912]{2,1,0:T(8,128)(2,1)} %pad_maximum_fusion.2.mine), custom_call_target="tpu_custom_call" | custom-call | tf_op jit(solution)/shard_map/pallas_call | solution.py:210
  147.7 3.5 %bitcast_convert_fusion = f32[768,912]{1,0:T(8,128)} fusion(bf16[8,96,912]{2,1,0:T(8,128)(2,1)} %get-tuple-element.17), kind=kLoop, calls=%fused_computation.26 | loop fusion | flops 700416 | bytes 4202496 | tf_op jit(solution)/shard_map/convert_element_type | solution.py:525
  151.2 3.5 %copy.75 = f32[768,912]{0,1:T(8,128)} copy(f32[768,912]{1,0:T(8,128)} %bitcast_convert_fusion) | data formatting | bytes 5603328 | tf_op jit(solution)/shard_map/convert_element_type | solution.py:525
  154.7 2.9 maximum_add_fusion
  157.6 0.6 multiply_convert_fusion.1
  158.2 1.2 copy-done.7
  159.4 2.0 fusion
  161.4 2.0 fusion.2
  163.4 2.0 fusion.1
  165.4 1.6 convolution_convert_fusion.1
  167.1 1.6 fusion.18
  168.7 1.8 add_convert_fusion
  170.6 2.8 pad_maximum_fusion.part
  173.3 4.6 %convolution_convert_fusion = bf16[3584,912]{0,1:T(8,128)(2,1)} fusion(bf16[128,3584]{1,0:T(8,128)(2,1)S(1)} %copy-done.3, bf16[128,3584]{1,0:T(8,128)(2,1)S(1)} %copy-done.2, bf16[128,304]{0,1:T(8,128)(2,1)S(1)} %copy-done.15, bf16[128,304]{0,1:T(8,128)(2,1)S(1)} %copy-done.11, bf16[128,304]{0,1:T(8,128)(2,1)S(1)} %copy-done.17, ...), kind=kOutput, calls=%fused_computation | convolution fusion | flops 1682800640 | bytes 8683520 | tf_op jit(solution)/shard_map/dot_general | solution.py:34
  178.0 10.2 %copy.76 = bf16[3584,912]{1,0:T(8,128)(2,1)} copy(bf16[3584,912]{0,1:T(8,128)(2,1)} %convolution_convert_fusion) | data formatting | bytes 13074432 | tf_op jit(solution)/shard_map/convert_element_type | solution.py:523
  188.2 87.4 %shard_map.163 = (bf16[4,48,1792]{2,1,0:T(8,128)(2,1)}, bf16[112,912]{1,0:T(8,128)(2,1)}) custom-call(bf16[8,4,48,1792]{3,2,1,0:T(8,128)(2,1)} %pad_maximum_fusion.part, bf16[4,4,2,112,912]{4,3,2,1,0:T(8,128)(2,1)} %bitcast.95), custom_call_target="tpu_custom_call" | custom-call | tf_op jit(solution)/shard_map/pallas_call | solution.py:351
  275.6 1.2 fusion.66
  276.8 1.1 slice_bitcast_fusion
  278.0 0.7 copy.79
  278.7 0.7 copy.78
  279.5 0.7 copy.77
  281.5 0.8 copy-done.4
  282.2 0.4 fusion.4
  282.8 47.9 %shard_map.164 = (bf16[8,16,3584]{2,1,0:T(8,128)(2,1)S(1)}, bf16[8,16,3584]{2,1,0:T(8,128)(2,1)S(1)}) custom-call(bf16[2,8,16,3584]{3,2,1,0:T(8,128)(2,1)S(1)} %pad_maximum_fusion.1.part, bf16[8,16,3584]{2,1,0:T(8,128)(2,1)S(1)} %bitcast.92, bf16[8,16,3584]{2,1,0:T(8,128)(2,1)S(1)} %bitcast.91), custom_call_target="tpu_custom_call" | custom-call | tf_op jit(solution)/shard_map/pallas_call | solution.py:437
  330.7 0.9 copy.84
  331.6 0.9 copy.85
  (67 shorter events, 3.4 us)
Async XLA Ops:
  0.6 90.3 %copy-start = (bf16[1,304,1792]{2,1,0:T(8,128)(2,1)S(1)}, bf16[1,304,1792]{2,1,0:T(8,128)(2,1)}, u32[]{:S(2)}) copy-start(bf16[1,304,1792]{2,1,0:T(8,128)(2,1)} %param.17) | copy-start | bytes 3268612
  0.6 10.6 %copy-start.2 = (bf16[128,3584]{1,0:T(8,128)(2,1)S(1)}, bf16[128,3584]{1,0:T(8,128)(2,1)}, u32[]{:S(2)}) copy-start(bf16[128,3584]{1,0:T(8,128)(2,1)} %param.11) | copy-start | bytes 2752516
  11.5 67.0 %copy-start.3 = (bf16[128,3584]{1,0:T(8,128)(2,1)S(1)}, bf16[128,3584]{1,0:T(8,128)(2,1)}, u32[]{:S(2)}) copy-start(bf16[128,3584]{1,0:T(8,128)(2,1)} %param.10) | copy-start | bytes 2752516
  78.5 6.3 %copy-start.18 = (bf16[4,4,2,112,912]{4,3,2,1,0:T(8,128)(2,1)S(1)}, bf16[4,4,2,112,912]{4,3,2,1,0:T(8,128)(2,1)}, u32[]{:S(2)}) copy-start(bf16[4,4,2,112,912]{4,3,2,1,0:T(8,128)(2,1)} %get-tuple-element.15) | copy-start | bytes 19611652
  84.6 4.3 %slice-start = ((s8[5505024]{0:T(1024)(128)(4,1)}), s8[4194304]{0:T(1024)(128)(4,1)S(1)}, s32[]{:S(2)}) async-start(s8[5505024]{0:T(1024)(128)(4,1)} %bitcast.97), calls=%async_computation | async-start | bytes 8388608
  84.7 4.1 %copy-start.12 = (bf16[128,304]{0,1:T(8,128)(2,1)}, bf16[128,304]{0,1:T(8,128)(2,1)S(1)}, u32[]{:S(2)}) copy-start(bf16[128,304]{0,1:T(8,128)(2,1)S(1)} %get-tuple-element.63) | copy-start | bytes 233476
  84.7 4.1 %copy-start.14 = (bf16[128,304]{0,1:T(8,128)(2,1)}, bf16[128,304]{0,1:T(8,128)(2,1)S(1)}, u32[]{:S(2)}) copy-start(bf16[128,304]{0,1:T(8,128)(2,1)S(1)} %get-tuple-element.64) | copy-start | bytes 233476
  84.7 4.1 %copy-start.16 = (bf16[128,304]{0,1:T(8,128)(2,1)}, bf16[128,304]{0,1:T(8,128)(2,1)S(1)}, u32[]{:S(2)}) copy-start(bf16[128,304]{0,1:T(8,128)(2,1)S(1)} %get-tuple-element.65) | copy-start | bytes 233476
  84.8 4.1 %copy-start.10 = (bf16[128,304]{0,1:T(8,128)(2,1)}, bf16[128,304]{0,1:T(8,128)(2,1)S(1)}, u32[]{:S(2)}) copy-start(bf16[128,304]{0,1:T(8,128)(2,1)S(1)} %broadcast_in_dim.31) | copy-start | bytes 233476
  84.8 4.1 %slice-start.1 = ((s8[5505024]{0:T(1024)(128)(4,1)}), s8[1310720]{0:T(1024)(128)(4,1)S(1)}, s32[]{:S(2)}) async-start(s8[5505024]{0:T(1024)(128)(4,1)} %bitcast.97), calls=%async_computation.1 | async-start | bytes 2621440
  90.9 2.2 copy-start.6
  157.6 1.8 copy-start.7
  159.4 2.0 copy-start.5
  165.4 1.6 copy-start.8
  167.1 1.6 copy-start.9
  170.5 2.8 copy-start.11
  170.5 2.8 copy-start.13
  170.5 2.8 copy-start.15
  170.5 2.8 copy-start.17
  280.2 2.0 copy-start.4
  282.8 49.7 %copy-start.1 = (bf16[1,304,1792]{2,1,0:T(8,128)(2,1)S(1)}, bf16[1,304,1792]{2,1,0:T(8,128)(2,1)}, u32[]{:S(2)}) copy-start(bf16[1,304,1792]{2,1,0:T(8,128)(2,1)} %param.17) | copy-start | bytes 3268612

commit v2 on v1

v2 whole, which is shorter than its diff:
```python
import functools

import jax
import jax.numpy as jnp
from jax import lax
from jax.experimental import pallas as pl
from jax.experimental.pallas import tpu as pltpu
from jax.sharding import PartitionSpec as P

MESH = pl.DeviceIdType.MESH
BF = jnp.bfloat16
F32 = jnp.float32
HBM = pl.BlockSpec(memory_space=pl.ANY)
VMEM = pl.BlockSpec(memory_space=pltpu.VMEM)
DMA = pltpu.SemaphoreType.DMA
ROWS_A = pl.ds(0, 48)
ROWS_B = pl.ds(48, 64)


def silu_pair(values):
    logistic = jax.nn.sigmoid(values)
    return (values * logistic, logistic * (1.0 + values * (1.0 - logistic)))


def product(left, right):
    return jnp.dot(left, right, preferred_element_type=F32)


def times_transposed(left, right):
    return lax.dot_general(left, right, (((1,), (1,)), ((), ())), preferred_element_type=F32)


def transposed_times(left, right):
    return lax.dot_general(left, right, (((0,), (0,)), ((), ())), preferred_element_type=F32)


def place():
    dp, e, z = lax.axis_index("dp"), lax.axis_index("expert"), lax.axis_index("tensor")
    return dp * 2 + e // 8, (e // 2) % 4, e % 2, z


def device(y, x, c, z):
    return (y // 2, (y % 2) * 8 + x * 2 + c, z)


def dispatch_dest(y, x, c, z, j):
    return (y + j) % 4, (x + z // 2 + 2 * (j % 2)) % 4, (c + z) % 2


def dispatch_source(y, x, c, z, j):
    return (y + 4 - j) % 4, (x + 8 - z // 2 - 2 * (j % 2)) % 4, (c + z) % 2


def remote(src, dst, send_sem, recv_sem, dev):
    return pltpu.make_async_remote_copy(
        src_ref=src, dst_ref=dst, send_sem=send_sem, recv_sem=recv_sem, device_id=dev, device_id_type=MESH
    )


def greet(devices, conditional=()):
    barrier = pltpu.get_barrier_semaphore()
    for dev in devices:
        pl.semaphore_signal(barrier, inc=1, device_id=dev, device_id_type=MESH)
    for cond, dev in conditional:
        @pl.when(cond)
        def _():
            pl.semaphore_signal(barrier, inc=1, device_id=dev, device_id_type=MESH)
    count = jnp.int32(len(devices))
    for cond, dev in conditional:
        count = count + jnp.where(cond, jnp.int32(1), jnp.int32(0))
    pl.semaphore_wait(barrier, count)


def add_into(dst, *others):
    total = dst[...].astype(F32)
    for other in others:
        total = total + other[...].astype(F32)
    dst[...] = total.astype(BF)


ORDER = (0, -1, 1, -2, 2, -3, 3, 4)


def layer_kernel(
    send, w, gate, up, down, tokens, cots,
    ret, dgrad, ggrad, ugrad, lgrad, dpart,
    recv, full, cr, mine, theirs, via, acts, spread, part, rr, ra, rb, rc, rd,
    dsp_s, dsp_r, ag_s, ag_r, loc, da_s, da_r, near_s, near_r, far_s, far_r,
    ring_s, ring_r, ret_s, ret_r, d_s, d_r,
):
    y, x, c, z = place()
    hid = gate.shape[1]
    right, left = device(y, x, c, (z + 1) % 8), device(y, x, c, (z + 7) % 8)
    xi = [(x + i) % 4 for i in (1, 2, 3)]
    yi = [(y + i) % 4 for i in (1, 2, 3)]
    xs = [device(y, i, c, z) for i in xi]
    ys = [device(i, x, c, z) for i in yi]
    above, below = ys[0], ys[2]
    other = device(y, x, 1 - c, z)
    dests = [dispatch_dest(y, x, c, z, j) for j in range(4)]
    sources = [dispatch_source(y, x, c, z, j) for j in range(4)]
    greet(
        [device(*s, z) for s in sources[1:]] + [device(*d, z) for d in dests[1:]] + xs + ys + [other, left, right],
        [(z != 0, device(*sources[0], z)), (z != 0, device(*dests[0], z))],
    )


    def disp(j):
        return remote(send.at[(y + j) % 4], recv.at[z, y], dsp_s.at[j], dsp_r.at[j], device(*dests[j], z))

    here = pltpu.make_async_copy(send.at[y], recv.at[z, y], dsp_r.at[0])

    def carry(direction, t, j):
        origin = (z + 9 - t) % 8 if direction == 0 else (z + t - 1) % 8
        k = (y + 4 - j) % 4
        return remote(
            recv.at[origin, k], recv.at[origin, k],
            ag_s.at[direction, t - 1, j], ag_r.at[direction, t - 1, j], (right, left)[direction],
        )

    def carried(direction, t):
        return range(4) if t < 4 else ((0, 1), (2, 3))[direction]

    @pl.when(z == 0)
    def _():
        here.start()

    @pl.when(z != 0)
    def _():
        disp(0).start()

    for j in (1, 2, 3):
        disp(j).start()

    own = pltpu.make_async_copy(w, full.at[y, x, c], loc.at[0])
    own.start()
    one_a = [remote(w.at[ROWS_A], full.at[y, x, c, ROWS_A], da_s.at[0, i], da_r.at[0, i], xs[i]) for i in range(3)]
    one_b = [remote(w.at[ROWS_B], full.at[y, x, c, ROWS_B], da_s.at[1, i], da_r.at[1, i], ys[i]) for i in range(3)]
    two_a = [
        remote(full.at[y, :, c, ROWS_A], full.at[y, :, c, ROWS_A], da_s.at[2, i], da_r.at[2, i], ys[i])
        for i in range(3)
    ]
    two_b = [
        remote(full.at[:, x, c, ROWS_B], full.at[:, x, c, ROWS_B], da_s.at[3, i], da_r.at[3, i], xs[i])
        for i in range(3)
    ]
    three = [remote(full.at[i, :, c], full.at[i, :, c], da_s.at[4, i], da_r.at[4, i], other) for i in range(4)]
    for copy in one_a + one_b:
        copy.start()


    def block(r):
        return (z + 8 + ORDER[r]) % 8

    def near(r, h):
        return remote(
            mine.at[block(r), h], via.at[block(r), h], near_s.at[r, h], near_r.at[r, h], (above, below)[h]
        )

    def far(r, h):
        return remote(
            via.at[block(r), h], theirs.at[block(r), h], far_s.at[r, h], far_r.at[r, h], (above, below)[h]
        )

    def pre_block(r):
        b = block(r)
        rows = recv[b].reshape(192, recv.shape[3])
        results = (product(rows, gate[...]), product(rows, up[...]), times_transposed(rows, down[...]))
        for q in range(3):
            first = 24 if q == 2 else 0
            value = results[q].reshape(4, 48, hid)[:, first : first + 24].reshape(2, 48, hid)
            mine[b, :, q] = value.astype(BF)
        for h in (0, 1):
            near(r, h).start()

    def relay(r):
        for h in (0, 1):
            near(r, h).wait_recv()
            far(r, h).start()

    for j in range(4):
        if j == 0:
            @pl.when(z == 0)
            def _():
                here.wait()

            @pl.when(z != 0)
            def _():
                disp(0).wait_recv()
        else:
            disp(j).wait_recv()
        carry(0, 1, j).start()
        carry(1, 1, j).start()
    own.wait()
    for copy in one_a + one_b:
        copy.wait_recv()
    for copy in two_a + two_b:
        copy.start()
    pre_block(0)

    def carry_step(t):
        for j in range(4):
            for direction in (0, 1):
                carry(direction, t - 1, j).wait_recv()
                if j in carried(direction, t):
                    carry(direction, t, j).start()


    def dense_forward():
        both = jnp.concatenate([tokens[...], cots[...]], axis=0)
        pre = product(both, full[...].reshape(both.shape[1], 3 * hid))
        active, slope = silu_pair(pre[:128, :hid])
        pre_up = pre[:128, hid : 2 * hid]
        grad_act = pre[128:, 2 * hid :]
        zeros = jnp.zeros((128, hid), F32)
        spread[0:128, :] = jnp.concatenate([zeros, zeros, active * pre_up], axis=1).astype(BF)
        spread[128:256, :] = jnp.concatenate(
            [grad_act * pre_up * slope, grad_act * active, zeros], axis=1
        ).astype(BF)

        @pl.loop(0, 4)
        def _(i):
            rows = full[i].reshape(896, 3 * hid)
            dpart[:, pl.ds(pl.multiple_of(i * 896, 128), 896)] = times_transposed(spread[...], rows).astype(BF)

    def dense_weights():
        @pl.loop(0, 4)
        def _(i):
            cols = pl.ds(pl.multiple_of(i * 896, 128), 896)
            value = transposed_times(cots[:, cols], spread[0:128, :])
            value = value + transposed_times(tokens[:, cols], spread[128:256, :])
            full[i] = value.astype(BF).reshape(4, 2, 112, 3 * hid)

    carry_step(2)
    pre_block(1)
    pre_block(2)
    relay(0)
    for copy in two_a + two_b:
        copy.wait_recv()
    for copy in three:
        copy.start()
    carry_step(3)
    pre_block(3)
    pre_block(4)
    relay(1)
    relay(2)
    for copy in three:
        copy.wait_recv()
    dense_forward()
    carry_step(4)
    pre_block(5)
    pre_block(6)
    relay(3)
    relay(4)
    for copy in one_a + one_b + two_a + two_b + three:
        copy.wait_send()
    for direction in (0, 1):
        for j in carried(direction, 4):
            carry(direction, 4, j).wait_recv()
    pre_block(7)
    relay(5)
    relay(6)
    dense_weights()
    relay(7)


    def results_block(r):
        b = block(r)
        for h in (0, 1):
            far(r, h).wait_recv()
        pre = [mine[b, :, q].astype(F32) + theirs[b, :, q].astype(F32) for q in range(3)]
        active, slope = silu_pair(pre[0])
        zeros = jnp.zeros((4, 24, hid), F32)
        grad_gate = (pre[2] * pre[1] * slope).reshape(4, 24, hid)
        grad_up = (pre[2] * active).reshape(4, 24, hid)
        hidden = (active * pre[1]).reshape(4, 24, hid)
        acts[0, b] = jnp.concatenate([grad_gate, zeros], axis=1).astype(BF)
        acts[1, b] = jnp.concatenate([grad_up, zeros], axis=1).astype(BF)
        acts[2, b] = jnp.concatenate([zeros, hidden], axis=1).astype(BF)
        value = times_transposed(acts[0, b].reshape(192, hid), gate[...])
        value = value + times_transposed(acts[1, b].reshape(192, hid), up[...])
        value = value + product(acts[2, b].reshape(192, hid), down[...])
        part[b] = value.astype(BF).reshape(part.shape[1:])


    def target(direction, u):
        return (z + 5 - u) % 8 if direction == 0 else (z + 3 + u) % 8

    def members(direction, u):
        return range(4) if u > 1 else ((0, 1), (2, 3))[direction]

    def hop(direction, u, k):
        fresh = u == 1 or (u == 2 and k not in members(direction, 1))
        src = part.at[target(direction, u), k] if fresh else rr.at[direction, u - 2, k]
        return remote(
            src, rr.at[direction, u - 1, k],
            ring_s.at[direction, u - 1, k], ring_r.at[direction, u - 1, k], (right, left)[direction],
        )

    def ring_step(u):
        for k in range(4):
            for direction in (0, 1):
                if u == 2 and k not in members(direction, 1):
                    continue
                hop(direction, u - 1, k).wait_recv()
                add_into(rr.at[direction, u - 2, k], part.at[target(direction, u), k])
                hop(direction, u, k).start()


    d_one = [remote(full.at[i, :, 1 - c], cr.at[i], d_s.at[0, i], d_r.at[0, i], other) for i in range(4)]
    d_two_a = [remote(cr.at[yi[i], :, ROWS_A], ra.at[i], d_s.at[1, i], d_r.at[1, i], ys[i]) for i in range(3)]
    d_two_b = [remote(cr.at[:, xi[i], ROWS_B], rb.at[i], d_s.at[2, i], d_r.at[2, i], xs[i]) for i in range(3)]
    d_three_a = [remote(cr.at[y, xi[i], ROWS_A], rc.at[i], d_s.at[3, i], d_r.at[3, i], xs[i]) for i in range(3)]
    d_three_b = [remote(cr.at[yi[i], x, ROWS_B], rd.at[i], d_s.at[4, i], d_r.at[4, i], ys[i]) for i in range(3)]

    for copy in d_one:
        copy.start()
    results_block(7)
    for direction in (0, 1):
        for k in members(direction, 1):
            hop(direction, 1, k).start()
    results_block(5)
    results_block(6)
    for direction in (0, 1):
        for k in range(4):
            if k not in members(direction, 1):
                hop(direction, 2, k).start()
    for copy in d_one:
        copy.wait_recv()

    @pl.loop(0, 16)
    def _(i):
        add_into(cr.at[i // 4, i % 4], full.at[i // 4, i % 4, c])

    for copy in d_two_a + d_two_b:
        copy.start()
    ring_step(2)
    results_block(3)
    results_block(4)
    for copy in d_two_a + d_two_b:
        copy.wait_recv()

    @pl.loop(0, 4)
    def _(i):
        add_into(cr.at[y, i, ROWS_A], ra.at[0, i], ra.at[1, i], ra.at[2, i])
        add_into(cr.at[i, x, ROWS_B], rb.at[0, i], rb.at[1, i], rb.at[2, i])

    for copy in d_three_a + d_three_b:
        copy.start()
    ring_step(3)
    results_block(1)
    results_block(2)
    for copy in d_three_a + d_three_b:
        copy.wait_recv()
    add_into(cr.at[y, x, ROWS_A], rc.at[0], rc.at[1], rc.at[2])
    add_into(cr.at[y, x, ROWS_B], rd.at[0], rd.at[1], rd.at[2])
    dgrad[...] = cr[y, x]
    ring_step(4)
    results_block(0)


    @pl.loop(0, recv.shape[3] // 256)
    def _(i):
        cols = pl.ds(pl.multiple_of(i * 256, 256), 256)
        rows = recv[:, :, :, cols].reshape(1536, 256)
        ggrad[cols, :] = transposed_times(rows, acts[0].reshape(1536, hid)).astype(BF)
        ugrad[cols, :] = transposed_times(rows, acts[1].reshape(1536, hid)).astype(BF)
        lgrad[:, cols] = transposed_times(acts[2].reshape(1536, hid), rows).astype(BF)


    def home(j):
        return remote(
            rr.at[0, 3, (y + 4 - j) % 4], ret.at[y], ret_s.at[j], ret_r.at[j], device(*sources[j], z)
        )

    back = pltpu.make_async_copy(rr.at[0, 3, y], ret.at[y], ret_r.at[0])
    for k in range(4):
        hop(0, 4, k).wait_recv()
        hop(1, 4, k).wait_recv()
        add_into(rr.at[0, 3, k], rr.at[1, 3, k], part.at[z, k])

    @pl.when(z == 0)
    def _():
        back.start()

    @pl.when(z != 0)
    def _():
        home(0).start()

    for j in (1, 2, 3):
        home(j).start()

    @pl.when(z == 0)
    def _():
        back.wait()

    @pl.when(z != 0)
    def _():
        home(0).wait()
        disp(0).wait_send()

    for j in (1, 2, 3):
        home(j).wait()
        disp(j).wait_send()
    for direction in (0, 1):
        for t in (1, 2, 3, 4):
            for k in members(direction, t):
                hop(direction, t, k).wait_send()
            for j in carried(direction, t):
                carry(direction, t, j).wait_send()
    for r in range(8):
        for h in (0, 1):
            near(r, h).wait_send()
            far(r, h).wait_send()
    for copy in d_one + d_two_a + d_two_b + d_three_a + d_three_b:
        copy.wait_send()


def layer_call(send, w, gate, up, down, tokens, cots):
    half, hid = gate.shape
    lanes = w.shape[1]
    count, width = tokens.shape
    shape = jax.ShapeDtypeStruct
    swap = pltpu.VMEM((8, 2, 3, 48, hid), BF)
    rows = pltpu.VMEM((8, 4, 48, half), BF)
    return pl.pallas_call(
        layer_kernel,
        out_shape=(
            shape((4, 48, half), BF),
            shape((112, lanes), BF),
            shape((half, hid), BF),
            shape((half, hid), BF),
            shape((hid, half), BF),
            shape((2 * count, width), BF),
        ),
        in_specs=[HBM, HBM] + [VMEM] * 5,
        out_specs=(HBM,) + (VMEM,) * 5,
        scratch_shapes=[
            rows,
            pltpu.VMEM((4, 4, 2, 112, lanes), BF),
            pltpu.VMEM((4, 4, 112, lanes), BF),
            swap, swap, swap,
            pltpu.VMEM((3, 8, 4, 48, hid), BF),
            pltpu.VMEM((2 * count, lanes), BF),
            rows,
            pltpu.VMEM((2, 4, 4, 48, half), BF),
            pltpu.VMEM((3, 4, 48, lanes), BF),
            pltpu.VMEM((3, 4, 64, lanes), BF),
            pltpu.VMEM((3, 48, lanes), BF),
            pltpu.VMEM((3, 64, lanes), BF),
            DMA((4,)), DMA((4,)), DMA((2, 4, 4)), DMA((2, 4, 4)), DMA((1,)), DMA((5, 4)), DMA((5, 4)),
            DMA((8, 2)), DMA((8, 2)), DMA((8, 2)), DMA((8, 2)),
            DMA((2, 4, 4)), DMA((2, 4, 4)), DMA((4,)), DMA((4,)), DMA((5, 4)), DMA((5, 4)),
        ],
        compiler_params=pltpu.CompilerParams(
            collective_id=0, has_side_effects=True, vmem_limit_bytes=62 * 1024 * 1024
        ),
    )(send, w, gate, up, down, tokens, cots)


def finish_kernel(part, tokens, cots, out, back, rr, rs_s, rs_r, ag_s, ag_r):
    y, x, c, z = place()
    right, left = device(y, x, c, (z + 1) % 8), device(y, x, c, (z + 7) % 8)
    greet([left, right])
    outs = (out, back)

    def target(direction, u):
        return (z + 5 - u) % 8 if direction == 0 else (z + 3 + u) % 8

    def hop(direction, u, q):
        src = part.at[q, target(direction, u)] if (u == 1 or (u == 2 and q != direction)) else rr.at[direction, u - 2, q]
        return remote(
            src, rr.at[direction, u - 1, q],
            rs_s.at[direction, u - 1, q], rs_r.at[direction, u - 1, q], (right, left)[direction],
        )

    def spread(direction, t, q):
        origin = (z + 9 - t) % 8 if direction == 0 else (z + t - 1) % 8
        return remote(
            outs[q].at[origin], outs[q].at[origin],
            ag_s.at[direction, t - 1, q], ag_r.at[direction, t - 1, q], (right, left)[direction],
        )

    for direction in (0, 1):
        hop(direction, 1, direction).start()
    for direction in (0, 1):
        hop(direction, 2, 1 - direction).start()
    for u in (2, 3, 4):
        for q in (0, 1):
            for direction in (0, 1):
                if u == 2 and q != direction:
                    continue
                hop(direction, u - 1, q).wait_recv()
                add_into(rr.at[direction, u - 2, q], part.at[q, target(direction, u)])
                hop(direction, u, q).start()
    for q in (0, 1):
        hop(0, 4, q).wait_recv()
        hop(1, 4, q).wait_recv()
        total = rr[0, 3, q].astype(F32) + rr[1, 3, q].astype(F32) + part[q, z].astype(F32)
        total = total + (tokens, cots)[q][z].astype(F32)
        outs[q][z] = total.astype(BF)
        for direction in (0, 1):
            spread(direction, 1, q).start()
    for t in (2, 3, 4):
        for q in (0, 1):
            for direction in (0, 1):
                spread(direction, t - 1, q).wait_recv()
                if t < 4 or q == direction:
                    spread(direction, t, q).start()
    for direction in (0, 1):
        spread(direction, 4, direction).wait_recv()
    for direction in (0, 1):
        for u in (1, 2, 3, 4):
            for q in (0, 1):
                if u > 1 or q == direction:
                    hop(direction, u, q).wait_send()
                if u < 4 or q == direction:
                    spread(direction, u, q).wait_send()


def finish_call(part, tokens, cots):
    width = part.shape[3]
    shape = jax.ShapeDtypeStruct((8, 16, width), BF)
    return pl.pallas_call(
        finish_kernel,
        out_shape=(shape, shape),
        in_specs=[VMEM, VMEM, VMEM],
        out_specs=(VMEM, VMEM),
        scratch_shapes=[
            pltpu.VMEM((2, 4, 2, 16, width), BF),
            DMA((2, 4, 2)), DMA((2, 4, 2)), DMA((2, 4, 2)), DMA((2, 4, 2)),
        ],
        compiler_params=pltpu.CompilerParams(
            collective_id=3, has_side_effects=True, vmem_limit_bytes=40 * 1024 * 1024
        ),
    )(part, tokens.reshape(8, 16, width), cots.reshape(8, 16, width))


def shards(
    tokens,
    cotangent,
    dense_gate,
    dense_up,
    dense_down,
    expert_gate,
    expert_up,
    expert_down,
    expert_ids,
    route_weights,
):
    count, width = tokens.shape
    half = width // 2
    hid = dense_gate.shape[1]
    experts, cap = 16, 24
    y, x, c, z = place()

    flat_ids = expert_ids.reshape(-1)
    onehot = (flat_ids[:, None] == jnp.arange(experts, dtype=jnp.int32)[None, :]).astype(jnp.int32)
    earlier = jnp.cumsum(onehot, axis=0) - onehot
    placed = (flat_ids * cap + jnp.sum(earlier * onehot, axis=1)).reshape(count, 2)

    y_d = jnp.arange(4, dtype=jnp.int32)
    x_d = (x + z // 2 + 2 * ((y_d + y) % 2)) % 4
    e_d = (y_d % 2) * 8 + x_d * 2 + (c + z) % 2
    slots = (e_d[:, None] * cap + jnp.arange(cap, dtype=jnp.int32)[None, :]).reshape(-1)
    hits = slots[:, None, None] == placed[None, :, :]
    select = jnp.any(hits, axis=2).astype(BF)
    weighted = jnp.sum(jnp.where(hits, route_weights[None, :, :], 0.0), axis=2)
    slot_weight = jnp.sum(weighted, axis=1)

    low, high = slice(0, 2 * cap), slice(2 * cap, 4 * cap)

    def picked(values):
        return jnp.concatenate(
            [product(select[low], values[:, :half]), product(select[high], values[:, half:])], axis=0
        )

    send_rows = picked(tokens).astype(BF).reshape(4, cap, half)
    send_cots = (picked(cotangent) * slot_weight[:, None]).astype(BF).reshape(4, cap, half)
    send = jnp.concatenate([send_rows, send_cots], axis=1)
    dense_cat = jnp.concatenate([dense_gate, dense_up, dense_down.T], axis=1)
    ret, dense_grad, gate_grad, up_grad, down_grad, dense_part = layer_call(
        send, dense_cat, expert_gate[0], expert_up[0], expert_down[0], tokens, cotangent
    )

    place_back = select.reshape(2, 2 * cap, count)
    place_out = weighted.astype(BF).reshape(2, 2 * cap, count)
    ret_back = ret[:, :cap].reshape(2, 2 * cap, half)
    ret_out = ret[:, cap:].reshape(2, 2 * cap, half)
    moe_out = jnp.concatenate([transposed_times(place_out[h], ret_out[h]) for h in (0, 1)], axis=1)
    moe_back = jnp.concatenate([transposed_times(place_back[h], ret_back[h]) for h in (0, 1)], axis=1)
    total = (dense_part.astype(F32).reshape(2, count, width) + jnp.stack([moe_out, moe_back])).astype(BF)
    output, input_grad = finish_call(total.reshape(2, 8, 16, width), tokens, cotangent)
    return (
        output.reshape(count, width),
        input_grad.reshape(count, width),
        dense_grad[:, :hid],
        dense_grad[:, hid : 2 * hid],
        dense_grad[:, 2 * hid :].T,
        gate_grad[None],
        up_grad[None],
        down_grad[None],
    )


def solution(mesh):
    in_specs = (
        P(("dp", "expert"), None),
        P(("dp", "expert"), None),
        P(("dp", "expert"), "tensor"),
        P(("dp", "expert"), "tensor"),
        P("tensor", ("dp", "expert")),
        P("expert", "dp", "tensor"),
        P("expert", "dp", "tensor"),
        P("expert", "tensor", "dp"),
        P(("dp", "expert"), None),
        P(("dp", "expert"), None),
    )
    out_specs = (
        P(("dp", "expert"), None),
        P(("dp", "expert"), None),
        P(("dp", "expert"), "tensor"),
        P(("dp", "expert"), "tensor"),
        P("tensor", ("dp", "expert")),
        P("expert", "dp", "tensor"),
        P("expert", "dp", "tensor"),
        P("expert", "tensor", "dp"),
    )
    return jax.shard_map(shards, mesh=mesh, in_specs=in_specs, out_specs=out_specs, check_vma=False)
```

time: 333 us -> 241 us (0.72)
  matrix products: 40.5 us -> 4.17 us
  Pallas kernels: 239 us -> 211 us
  local copies, waits for them, and re-layouts: 34.4 us -> 17.8 us
  other arithmetic: 17.9 us -> 4.48 us
    pallas_call x3 -> x1, Pallas kernels: 191 us -> 168 us  [layer_call(): pl.pallas_call(layer_kernel, out_shape=(shape((4, 48, half), BF), shape((...]
    dot_general x8 -> x4, matrix products: 18.9 us -> 2.91 us  [product(): return jnp.dot(left, right, preferred_element_type=F32)]
    convert_element_type x2 -> x0, local copies, waits for them, and re-layouts: 13.7 us -> none  [the longest x1 10.2 us: shards(): transposed_times(swapped, spread).astype(BF).reshape(4, 4, 2, 112, 3 * hid)]
    dot_general x8 -> x4, matrix products: 11.9 us -> 1.26 us  [transposed_times(): lax.dot_general(left, right, (((0,), (0,)), ((), ())), preferred_element_...]
    dot_general x4 -> x0, matrix products: 9.63 us -> none  [times_transposed(): lax.dot_general(left, right, (((1,), (1,)), ((), ())), preferred_element_...]
    concatenate x2, other arithmetic: 5.92 us -> 0.34 us  [the longest x1 0.17 us: shards(): jnp.concatenate([transposed_times(place_out[h], ret_out[h]) for h in (0,...]
    unnamed x51 -> x40, local copies, waits for them, and re-layouts: 10 us -> 15.6 us
    another operation x4 -> x1, local copies, waits for them, and re-layouts: 5.48 us -> 0.01 us
where the time goes in v2:
time: 241 us; the launch traced here: 238 us
  Pallas kernels  211 us (88%)
  local copies, waits for them, and re-layouts  17.8 us (7%)
  other arithmetic  4.48 us (2%)
  matrix products  4.17 us (2%)
    pallas_call x1, Pallas kernels, layer_call(): pl.pallas_call(layer_kernel, out_shape=(shape((4, 48, half), BF), shape((...  168 us
    pallas_call x1, Pallas kernels, finish_call(): pl.pallas_call(finish_kernel, out_shape=(shape, shape), in_specs=[VMEM, V...  43 us
    unnamed x40, local copies, waits for them, and re-layouts  15.6 us

profile of v2, /device:TPU:34, one launch (start us, length us, event | category | flops | bytes accessed | tf_op | source)
XLA Modules:
  0.0 238.5 jit_solution(13384658014856814192)
XLA Ops:
  0.7 0.1 iota_add_fusion
  0.8 0.1 add.133
  0.9 0.8 copy.62
  1.7 0.1 eq.51
  1.8 0.6 reduce-window.6
  2.4 0.2 slice_reduce_fusion
  2.7 0.1 eq.47
  2.8 0.1 fusion.9
  2.9 0.1 reduce_sum.30
  3.0 0.1 copy.65
  3.1 0.7 multiply_add_fusion
  3.8 0.1 compare_reduce_fusion
  3.9 1.3 fusion.1
  5.2 1.2 fusion.3
  6.5 0.2 select_reduce_fusion
  6.7 0.1 mul.62
  6.8 0.1 multiply_convert_fusion
  6.9 0.2 convolution_convert_fusion
  7.1 0.2 convolution_convert_fusion.1
  7.4 0.9 pad_maximum_fusion.3.send
  8.3 1.5 copy.69
  9.8 1.5 copy.70
  11.3 0.1 copy.66
  11.4 0.1 copy.67
  11.6 0.1 copy.68
  11.7 0.8 pad_maximum_fusion.5.w
  12.5 168.1 %shard_map.161 = (bf16[4,48,1792]{2,1,0:T(8,128)(2,1)}, bf16[112,912]{1,0:T(8,128)(2,1)}, bf16[1792,304]{1,0:T(8,128)(2,1)}, bf16[1792,304]{1,0:T(8,128)(2,1)}, ...) custom-call(bf16[4,48,1792]{2,1,0:T(8,128)(2,1)} %pad_maximum_fusion.3.send, bf16[112,912]{1,0:T(8,128)(2,1)} %pad_maximum_fusion.5.w, ...), custom_call_target="tpu_custom_call" | custom-call | tf_op jit(solution)/shard_map/pallas_call | solution.py:426
  180.6 1.2 fusion.30
  181.8 0.3 fusion.19
  182.1 0.3 fusion.21
  182.4 0.2 pad_maximum_fusion
  182.6 0.3 fusion.15
  182.9 0.3 fusion.11
  183.3 0.2 pad_maximum_fusion.1
  183.5 1.3 copy-done.3
  184.8 0.4 fusion.part
  185.2 0.7 copy-done
  186.0 0.3 copy-done.2
  186.2 43.0 %shard_map.162 = (bf16[8,16,3584]{2,1,0:T(8,128)(2,1)S(1)}, bf16[8,16,3584]{2,1,0:T(8,128)(2,1)S(1)}) custom-call(bf16[2,8,16,3584]{3,2,1,0:T(8,128)(2,1)S(1)} %fusion.part, bf16[8,16,3584]{2,1,0:T(8,128)(2,1)S(1)} %bitcast.47, bf16[8,16,3584]{2,1,0:T(8,128)(2,1)S(1)} %bitcast.46), custom_call_target="tpu_custom_call" | custom-call | tf_op jit(solution)/shard_map/pallas_call | solution.py:524
  229.3 2.5 %copy.74 = bf16[1,1792,304]{1,2,0:T(8,128)(2,1)} copy(bf16[1,1792,304]{2,1,0:T(8,128)(2,1)} %bitcast.57) | data formatting | bytes 2179072
  231.8 1.5 copy.75
  233.3 0.1 slice_bitcast_fusion
  233.4 0.7 copy.71
  234.1 0.7 copy.72
  234.9 0.7 copy.73
  235.6 0.9 copy.81
  236.6 0.9 copy.82
  237.5 1.0 copy.83
  (29 shorter events, 0.2 us)
Async XLA Ops:
  0.6 5.9 %copy-start.12 = (f32[128,2]{0,1:T(2,128)S(1)}, f32[128,2]{0,1:T(2,128)}, u32[]{:S(2)}) copy-start(f32[128,2]{0,1:T(2,128)} %param.19) | copy-start | bytes 3076
  3.9 3.0 %copy-start.1 = (bf16[128,3584]{1,0:T(8,128)(2,1)S(1)}, bf16[128,3584]{1,0:T(8,128)(2,1)}, u32[]{:S(2)}) copy-start(bf16[128,3584]{1,0:T(8,128)(2,1)} %tokens.1) | copy-start | bytes 2752516
  6.9 1.4 copy-start.5
  7.3 2.4 %copy-start.6 = (bf16[1,1792,304]{1,2,0:T(8,128)(2,1)S(1)}, bf16[1,1792,304]{1,2,0:T(8,128)(2,1)}, u32[]{:S(2)}) copy-start(bf16[1,1792,304]{1,2,0:T(8,128)(2,1)} %param.16) | copy-start | bytes 3268612
  9.8 1.5 copy-start.9
  9.8 1.7 copy-start.10
  9.8 1.8 copy-start.11
  183.3 1.5 copy-start.3
  184.8 1.2 copy-start
  184.8 1.5 copy-start.2
  229.3 2.5 %copy-start.4 = (bf16[1792,304]{1,0:T(8,128)(2,1)S(1)}, bf16[1792,304]{1,0:T(8,128)(2,1)}, u32[]{:S(2)}) copy-start(bf16[1792,304]{1,0:T(8,128)(2,1)} %get-tuple-element.22) | copy-start | bytes 3268612
  231.8 1.5 copy-start.8
  235.6 1.8 copy-start.7

commit v3 on v0

v3 whole, which is shorter than its diff:
```python
import functools

import jax
import jax.numpy as jnp
from jax import lax
from jax.experimental import pallas as pl
from jax.experimental.pallas import tpu as pltpu
from jax.sharding import PartitionSpec as P

MESH = pl.DeviceIdType.MESH
BF = jnp.bfloat16
F32 = jnp.float32
HBM = pl.BlockSpec(memory_space=pl.ANY)
VMEM = pl.BlockSpec(memory_space=pltpu.VMEM)
DMA = pltpu.SemaphoreType.DMA
ROWS_A = pl.ds(0, 48)
ROWS_B = pl.ds(48, 64)
ROWS_A0, ROWS_A1 = pl.ds(0, 16), pl.ds(16, 32)
ROWS_B0, ROWS_B1 = pl.ds(48, 32), pl.ds(80, 32)
LOW, HIGH = pl.ds(0, 2), pl.ds(2, 2)


def silu_pair(values):
    logistic = jax.nn.sigmoid(values)
    return (values * logistic, logistic * (1.0 + values * (1.0 - logistic)))


def product(left, right):
    return jnp.dot(left, right, preferred_element_type=F32)


def times_transposed(left, right):
    return lax.dot_general(left, right, (((1,), (1,)), ((), ())), preferred_element_type=F32)


def transposed_times(left, right):
    return lax.dot_general(left, right, (((0,), (0,)), ((), ())), preferred_element_type=F32)


def place():
    dp, e, z = lax.axis_index("dp"), lax.axis_index("expert"), lax.axis_index("tensor")
    return dp * 2 + e // 8, (e // 2) % 4, e % 2, z


def device(y, x, c, z):
    return (y // 2, (y % 2) * 8 + x * 2 + c, z)


def dispatch_dest(y, x, c, owner, j):
    return (y + j) % 4, (x + owner // 2 + 2 * (j % 2)) % 4, (c + owner) % 2


def dispatch_source(y, x, c, owner, j):
    return (y + 4 - j) % 4, (x + 8 - owner // 2 - 2 * (j % 2)) % 4, (c + owner) % 2


def remote(src, dst, send_sem, recv_sem, dev):
    return pltpu.make_async_remote_copy(
        src_ref=src, dst_ref=dst, send_sem=send_sem, recv_sem=recv_sem, device_id=dev, device_id_type=MESH
    )


def greet(devices, conditional=()):
    barrier = pltpu.get_barrier_semaphore()
    for dev in devices:
        pl.semaphore_signal(barrier, inc=1, device_id=dev, device_id_type=MESH)
    for cond, dev in conditional:
        @pl.when(cond)
        def _():
            pl.semaphore_signal(barrier, inc=1, device_id=dev, device_id_type=MESH)
    count = jnp.int32(len(devices))
    for cond, dev in conditional:
        count = count + jnp.where(cond, jnp.int32(1), jnp.int32(0))
    pl.semaphore_wait(barrier, count)


def add_into(dst, *others):
    total = dst[...].astype(F32)
    for other in others:
        total = total + other[...].astype(F32)
    dst[...] = total.astype(BF)


ORDER = (0, 3, -3, 4, -1, 1, -2, 2)
DIRECT = 3
HOME = (0, 3)


def layer_kernel(
    sel, slot, tokens, cots, w, gate, up, down,
    back, out, dgrad, wgrad,
    send, wt, recv, full, cr, mine, theirs, via, acts, spread, part, rr, ra, rb, rc, rd, ret, tot, rz,
    wt_s, dsp_s, dsp_r, ag_s, ag_r, loc, da_s, da_r, near_s, near_r, far_s, far_r,
    ring_s, ring_r, ret_s, ret_r, d_s, d_r, rs_s, rs_r, fin_s, fin_r,
):
    y, x, c, z = place()
    hid, half = gate.shape
    right, left = device(y, x, c, (z + 1) % 8), device(y, x, c, (z + 7) % 8)
    xp, xm, yp, ym = (x + 1) % 4, (x + 3) % 4, (y + 1) % 4, (y + 3) % 4
    east, west = device(y, xp, c, z), device(y, xm, c, z)
    above, below = device(yp, x, c, z), device(ym, x, c, z)
    other = device(y, x, 1 - c, z)

    def block(r):
        return (z + 8 + ORDER[r]) % 8

    def dest(r, j):
        return device(*dispatch_dest(y, x, c, block(r), j), z)

    def source(r, j):
        return device(*dispatch_source(y, x, c, block(r), j), z)

    greet(
        [source(r, j) for r in range(DIRECT) for j in (1, 2, 3)]
        + [dest(r, j) for r in HOME for j in (1, 2, 3)]
        + [east, west, above, below, other, left, right],
        [(block(r) != 0, source(r, 0)) for r in range(DIRECT)] + [(block(r) != 0, dest(r, 0)) for r in HOME],
    )
    weights = [
        pltpu.make_async_copy(ref, wt.at[pl.ds(i * hid, hid)], wt_s.at[i]) for i, ref in enumerate((gate, up, down))
    ]
    for copy in weights:
        copy.start()


    def build(r):
        for h in (0, 1):
            cols = slice(h * half, (h + 1) * half)
            chosen = sel[h, r].reshape(96, 256)
            value = product(chosen[:, :128], tokens[:, cols]) + product(chosen[:, 128:], cots[:, cols])
            send[h, r] = (value * slot[h, r].reshape(96, 1)).astype(BF).reshape(2, 48, half)

    def straight(j, r, src, dst, send_sem, recv_sem, dev, action):
        copy = remote(src, dst, send_sem, recv_sem, dev)
        if j:
            getattr(copy, action)()
            return

        @pl.when(block(r) == 0)
        def _():
            if action != "wait_send":
                stay = pltpu.make_async_copy(src, dst, recv_sem)
                stay.start() if action == "start" else stay.wait()

        @pl.when(block(r) != 0)
        def _():
            getattr(copy, action)()

    def disp(r, j, action):
        y_d = (y + j) % 4
        straight(
            j, r, send.at[y_d // 2, r, y_d % 2], recv.at[block(r), y], dsp_s.at[r, j], dsp_r.at[r, j], dest(r, j), action
        )

    def carried(direction, t):
        return range(4) if t < 3 else ((0, 1), (2, 3))[direction]

    def carry_step(t):
        for j in range(4):
            for direction in (0, 1):
                carry(direction, t - 1, j).wait_recv()
                if j in carried(direction, t):
                    carry(direction, t, j).start()

    def carry(direction, t, j):
        ahead = t if t < 3 else 4
        origin = (z + 9 - ahead) % 8 if direction == 0 else (z + ahead - 1) % 8
        k = (y + 4 - j) % 4
        return remote(
            recv.at[origin, k], recv.at[origin, k],
            ag_s.at[direction, t - 1, j], ag_r.at[direction, t - 1, j], (right, left)[direction],
        )

    build(0)
    for j in range(4):
        disp(0, j, "start")
    for r in range(1, DIRECT):
        build(r)


    own = pltpu.make_async_copy(w, full.at[y, x, c], loc.at[0])
    own.start()

    def pass_on(stage, i, place_of, dev):
        return remote(place_of, place_of, da_s.at[stage, i], da_r.at[stage, i], dev)

    def first_send(i, rows, dev):
        return remote(w.at[rows], full.at[y, x, c, rows], da_s.at[0, i], da_r.at[0, i], dev)

    ga = [
        first_send(0, ROWS_A, east),
        first_send(1, ROWS_A, west),
        first_send(2, ROWS_B, above),
        first_send(3, ROWS_B, below),
    ]
    gb = [
        pass_on(1, 0, full.at[y, xm, c, ROWS_A0], east),
        pass_on(1, 1, full.at[y, xp, c, ROWS_A1], west),
        pass_on(1, 2, full.at[ym, x, c, ROWS_B0], above),
        pass_on(1, 3, full.at[yp, x, c, ROWS_B1], below),
    ]
    gc = [
        pass_on(2, 0, full.at[y, :, c, ROWS_A], above),
        pass_on(2, 1, full.at[y, :, c, ROWS_A], below),
        pass_on(2, 2, full.at[:, x, c, ROWS_B], east),
        pass_on(2, 3, full.at[:, x, c, ROWS_B], west),
    ]
    gd = [
        pass_on(3, 0, full.at[ym, LOW, c, ROWS_A], above),
        pass_on(3, 1, full.at[yp, HIGH, c, ROWS_A], below),
        pass_on(3, 2, full.at[LOW, xm, c, ROWS_B], east),
        pass_on(3, 3, full.at[HIGH, xp, c, ROWS_B], west),
    ]
    ge = [pass_on(4, i, full.at[i, :, c], other) for i in range(4)]

    def after(earlier, later):
        for copy in earlier:
            copy.wait_recv()
        for copy in later:
            copy.start()


    def near(r, h):
        return remote(
            mine.at[block(r), h], via.at[block(r), h], near_s.at[r, h], near_r.at[r, h], (above, below)[h]
        )

    def far(r, h):
        return remote(
            via.at[block(r), h], theirs.at[block(r), h], far_s.at[r, h], far_r.at[r, h], (above, below)[h]
        )

    def pre_block(r):
        b = block(r)
        value = times_transposed(recv[b].reshape(192, half), wt[...]).reshape(4, 48, 3 * hid)
        lane = lax.broadcasted_iota(jnp.int32, (4, 24, 3 * hid), 2)
        value = jnp.where(lane < 2 * hid, value[:, :24], value[:, 24:])
        mine[b] = value.reshape(2, 48, 3 * hid).astype(BF)
        for h in (0, 1):
            near(r, h).start()

    def relay(r):
        for h in (0, 1):
            near(r, h).wait_recv()
            far(r, h).start()


    def results_block(r):
        b = block(r)
        for h in (0, 1):
            far(r, h).wait_recv()
        pre = (mine[b].astype(F32) + theirs[b].astype(F32)).reshape(4, 24, 3 * hid)
        pre_up, grad_act = pre[:, :, hid : 2 * hid], pre[:, :, 2 * hid :]
        active, slope = silu_pair(pre[:, :, :hid])
        zeros = jnp.zeros((4, 24, hid), F32)
        first = jnp.concatenate([grad_act * pre_up * slope, grad_act * active, zeros], axis=2)
        second = jnp.concatenate([zeros, zeros, active * pre_up], axis=2)
        acts[b] = jnp.concatenate([first, second], axis=1).astype(BF)
        part[b] = product(acts[b].reshape(192, 3 * hid), wt[...]).astype(BF).reshape(4, 48, half)


    def dense_forward():
        both = jnp.concatenate([tokens[...], cots[...]], axis=0)
        pre = product(both, full[...].reshape(both.shape[1], 3 * hid))
        active, slope = silu_pair(pre[:128, :hid])
        pre_up = pre[:128, hid : 2 * hid]
        grad_act = pre[128:, 2 * hid :]
        zeros = jnp.zeros((128, hid), F32)
        spread[0:128, :] = jnp.concatenate(
            [grad_act * pre_up * slope, grad_act * active, zeros], axis=1
        ).astype(BF)
        spread[128:256, :] = jnp.concatenate([zeros, zeros, active * pre_up], axis=1).astype(BF)

        @pl.loop(0, 4)
        def _(i):
            rows = full[i].reshape(896, 3 * hid)
            value = times_transposed(spread[...], rows).astype(BF)
            tot[:, :, :, pl.ds(pl.multiple_of(i * 896, 128), 896)] = value.reshape(2, 8, 16, 896)

    def dense_weights():
        @pl.loop(0, 4)
        def _(i):
            cols = pl.ds(pl.multiple_of(i * 896, 128), 896)
            value = transposed_times(tokens[:, cols], spread[0:128, :])
            value = value + transposed_times(cots[:, cols], spread[128:256, :])
            full[i] = value.astype(BF).reshape(4, 2, 112, 3 * hid)


    def target(direction, v):
        return (z + 4 - v) % 8 if direction == 0 else (z + 4 + v) % 8

    def hop(direction, v, k):
        src = part.at[target(direction, 1), k] if v == 1 else rr.at[direction, v - 2, k]
        return remote(
            src, rr.at[direction, v - 1, k],
            ring_s.at[direction, v - 1, k], ring_r.at[direction, v - 1, k], (right, left)[direction],
        )

    def ring_step(v):
        for k in range(4):
            for direction in (0, 1):
                hop(direction, v - 1, k).wait_recv()
                add_into(rr.at[direction, v - 2, k], part.at[target(direction, v), k])
                hop(direction, v, k).start()

    def home(r, j, action):
        k = (y + 4 - j) % 4
        src = rr.at[0, 2, k] if r == 0 else part.at[block(r), k]
        straight(j, r, src, ret.at[r // 3, y], ret_s.at[r // 3, j], ret_r.at[r // 3, j], source(r, j), action)


    def partial(stage, i, src, dst, dev):
        return remote(src, dst, d_s.at[stage, i], d_r.at[stage, i], dev)

    yo, xo = (y + 2) % 4, (x + 2) % 4
    s_one = [partial(0, i, full.at[i, :, 1 - c], cr.at[i], other) for i in range(4)]
    s_two = [
        partial(1, 0, cr.at[yo, LOW, ROWS_A], ra.at[0, LOW], above),
        partial(1, 1, cr.at[yo, HIGH, ROWS_A], ra.at[0, HIGH], below),
        partial(1, 2, cr.at[LOW, xo, ROWS_B], rb.at[0, LOW], east),
        partial(1, 3, cr.at[HIGH, xo, ROWS_B], rb.at[0, HIGH], west),
    ]
    s_three = [
        partial(2, 0, cr.at[yp, :, ROWS_A], ra.at[1], above),
        partial(2, 1, cr.at[ym, :, ROWS_A], ra.at[2], below),
        partial(2, 2, cr.at[:, xp, ROWS_B], rb.at[1], east),
        partial(2, 3, cr.at[:, xm, ROWS_B], rb.at[2], west),
    ]
    s_four = [
        partial(3, 0, cr.at[y, xo, ROWS_A0], rc.at[0, ROWS_A0], east),
        partial(3, 1, cr.at[y, xo, ROWS_A1], rc.at[0, ROWS_A1], west),
        partial(3, 2, cr.at[yo, x, ROWS_B0], rd.at[0, pl.ds(0, 32)], above),
        partial(3, 3, cr.at[yo, x, ROWS_B1], rd.at[0, pl.ds(32, 32)], below),
    ]
    s_five = [
        partial(4, 0, cr.at[y, xp, ROWS_A], rc.at[1], east),
        partial(4, 1, cr.at[y, xm, ROWS_A], rc.at[2], west),
        partial(4, 2, cr.at[yp, x, ROWS_B], rd.at[1], above),
        partial(4, 3, cr.at[ym, x, ROWS_B], rd.at[2], below),
    ]

    def scatter_two():
        for copy in s_one:
            copy.wait_recv()

        @pl.loop(0, 16)
        def _(i):
            add_into(cr.at[i // 4, i % 4], full.at[i // 4, i % 4, c])

        for copy in s_two:
            copy.start()

    def scatter_three():
        for copy in s_two:
            copy.wait_recv()

        @pl.loop(0, 2)
        def _(i):
            add_into(cr.at[yp, i, ROWS_A], ra.at[0, i])
            add_into(cr.at[ym, i + 2, ROWS_A], ra.at[0, i + 2])
            add_into(cr.at[i, xp, ROWS_B], rb.at[0, i])
            add_into(cr.at[i + 2, xm, ROWS_B], rb.at[0, i + 2])

        for copy in s_three:
            copy.start()

    def scatter_four():
        for copy in s_three:
            copy.wait_recv()

        @pl.loop(0, 4)
        def _(i):
            add_into(cr.at[y, i, ROWS_A], ra.at[1, i], ra.at[2, i])
            add_into(cr.at[i, x, ROWS_B], rb.at[1, i], rb.at[2, i])

        for copy in s_four:
            copy.start()

    def scatter_five():
        for copy in s_four:
            copy.wait_recv()
        add_into(cr.at[y, xp, ROWS_A0], rc.at[0, ROWS_A0])
        add_into(cr.at[y, xm, ROWS_A1], rc.at[0, ROWS_A1])
        add_into(cr.at[yp, x, ROWS_B0], rd.at[0, pl.ds(0, 32)])
        add_into(cr.at[ym, x, ROWS_B1], rd.at[0, pl.ds(32, 32)])
        for copy in s_five:
            copy.start()

    def scatter_end():
        for copy in s_five:
            copy.wait_recv()
        add_into(cr.at[y, x, ROWS_A], rc.at[1], rc.at[2])
        add_into(cr.at[y, x, ROWS_B], rd.at[1], rd.at[2])
        dgrad[...] = cr[y, x]


    def expert_weights(first, count):
        rows = acts[:, :, :, first : first + count].reshape(1536, count)
        wgrad[first : first + count, :] = transposed_times(rows, recv[...].reshape(1536, half)).astype(BF)


    outs = (back, out)

    def final_target(direction, u):
        return (z + 5 - u) % 8 if direction == 0 else (z + 3 + u) % 8

    def final_hop(direction, u, q):
        fresh = u == 1 or (u == 2 and q != direction)
        src = tot.at[q, final_target(direction, u)] if fresh else rz.at[direction, u - 2, q]
        return remote(
            src, rz.at[direction, u - 1, q],
            rs_s.at[direction, u - 1, q], rs_r.at[direction, u - 1, q], (right, left)[direction],
        )

    def final_step(u):
        for q in (0, 1):
            for direction in (0, 1):
                if u == 2 and q != direction:
                    continue
                final_hop(direction, u - 1, q).wait_recv()
                add_into(rz.at[direction, u - 2, q], tot.at[q, final_target(direction, u)])
                final_hop(direction, u, q).start()

    def share(direction, t, q):
        origin = (z + 9 - t) % 8 if direction == 0 else (z + t - 1) % 8
        return remote(
            outs[q].at[origin], outs[q].at[origin],
            fin_s.at[direction, t - 1, q], fin_r.at[direction, t - 1, q], (right, left)[direction],
        )


    for j in range(4):
        disp(0, j, "wait_recv")
        carry(0, 1, j).start()
        carry(1, 1, j).start()
    for r in range(1, DIRECT):
        for j in range(4):
            disp(r, j, "start")
    for copy in ga:
        copy.start()
    for copy in weights:
        copy.wait()
    pre_block(0)
    carry_step(2)
    after(ga, gb)
    for r in range(1, DIRECT):
        for j in range(4):
            disp(r, j, "wait_recv")
        pre_block(r)
    relay(0)
    pre_block(4)
    pre_block(5)
    own.wait()
    after(gb, gc)
    relay(1)
    relay(2)
    carry_step(3)
    for r in (1, 2):
        results_block(r)
        for k in range(4):
            hop(r - 1, 1, k).start()
    pre_block(6)
    pre_block(7)
    relay(4)
    relay(5)
    after(gc, gd)
    relay(6)
    relay(7)
    for direction in (0, 1):
        for j in carried(direction, 3):
            carry(direction, 3, j).wait_recv()
    pre_block(3)
    results_block(6)
    results_block(7)
    relay(3)
    ring_step(2)
    after(gd, ge)
    results_block(3)
    for j in range(4):
        home(3, j, "start")
    results_block(4)
    results_block(5)
    after(ge, ())
    dense_forward()
    ring_step(3)
    results_block(0)
    for copy in ga + gb + gc + gd + ge:
        copy.wait_send()
    dense_weights()
    for copy in s_one:
        copy.start()
    for k in range(4):
        hop(0, 3, k).wait_recv()
        hop(1, 3, k).wait_recv()
        add_into(rr.at[0, 2, k], rr.at[1, 2, k], part.at[z, k])
    for j in range(4):
        home(0, j, "start")
    scatter_two()
    expert_weights(0, 256)
    scatter_three()
    for i in range(1, 3):
        expert_weights(256 * i, 256)
    expert_weights(768, 3 * hid - 768)
    for r in HOME:
        for j in range(4):
            home(r, j, "wait_recv")
    for h in (0, 1):
        cols = slice(h * half, (h + 1) * half)
        value = jnp.zeros((256, half), F32)
        for i, r in enumerate(HOME):
            rows = ret[i, 2 * h : 2 * h + 2].reshape(96, half).astype(F32) * slot[h, r].reshape(96, 1)
            value = value + transposed_times(sel[h, r].reshape(96, 256), rows.astype(BF))
        value = value.reshape(2, 8, 16, half)
        tot[:, :, :, cols] = (tot[:, :, :, cols].astype(F32) + value).astype(BF)
    for direction in (0, 1):
        final_hop(direction, 1, direction).start()
    for direction in (0, 1):
        final_hop(direction, 2, 1 - direction).start()
    scatter_four()
    final_step(2)
    scatter_five()
    final_step(3)
    final_step(4)
    scatter_end()
    mine_rows = pl.ds(pl.multiple_of(z * 16, 16), 16)
    for q in (0, 1):
        final_hop(0, 4, q).wait_recv()
        final_hop(1, 4, q).wait_recv()
        total = rz[0, 3, q].astype(F32) + rz[1, 3, q].astype(F32) + tot[q, z].astype(F32)
        total = total + (cots, tokens)[q][mine_rows, :].astype(F32)
        outs[q][z] = total.astype(BF)
        for direction in (0, 1):
            share(direction, 1, q).start()
    for t in (2, 3, 4):
        for q in (0, 1):
            for direction in (0, 1):
                share(direction, t - 1, q).wait_recv()
                if t < 4 or q == direction:
                    share(direction, t, q).start()
    for direction in (0, 1):
        share(direction, 4, direction).wait_recv()


    for r in range(DIRECT):
        for j in range(4):
            disp(r, j, "wait_send")
    for r in HOME:
        for j in range(4):
            home(r, j, "wait_send")
    for r in range(8):
        for h in (0, 1):
            near(r, h).wait_send()
            far(r, h).wait_send()
    for direction in (0, 1):
        for k in range(4):
            for t in (1, 2, 3):
                if k in carried(direction, t):
                    carry(direction, t, k).wait_send()
            for v in (1, 2, 3):
                hop(direction, v, k).wait_send()
        for u in (1, 2, 3, 4):
            for q in (0, 1):
                if u > 1 or q == direction:
                    final_hop(direction, u, q).wait_send()
                if u < 4 or q == direction:
                    share(direction, u, q).wait_send()
    for copy in s_one + s_two + s_three + s_four + s_five:
        copy.wait_send()


def layer_call(sel, slot, tokens, cots, w, gate, up, down):
    hid, half = gate.shape
    lanes = w.shape[1]
    count, width = tokens.shape
    shape = jax.ShapeDtypeStruct
    swap = pltpu.VMEM((8, 2, 48, lanes), BF)
    rows = pltpu.VMEM((8, 4, 48, half), BF)
    return pl.pallas_call(
        layer_kernel,
        out_shape=(
            shape((8, 16, width), BF),
            shape((8, 16, width), BF),
            shape((112, lanes), BF),
            shape((lanes, half), BF),
        ),
        in_specs=[VMEM] * 4 + [HBM] * 4,
        out_specs=(VMEM,) * 4,
        scratch_shapes=[
            pltpu.VMEM((2, DIRECT, 2, 48, half), BF),
            pltpu.VMEM((lanes, half), BF),
            rows,
            pltpu.VMEM((4, 4, 2, 112, lanes), BF),
            pltpu.VMEM((4, 4, 112, lanes), BF),
            swap, swap, swap,
            pltpu.VMEM((8, 4, 48, lanes), BF),
            pltpu.VMEM((2 * count, lanes), BF),
            rows,
            pltpu.VMEM((2, 3, 4, 48, half), BF),
            pltpu.VMEM((3, 4, 48, lanes), BF),
            pltpu.VMEM((3, 4, 64, lanes), BF),
            pltpu.VMEM((3, 48, lanes), BF),
            pltpu.VMEM((3, 64, lanes), BF),
            pltpu.VMEM((len(HOME), 4, 48, half), BF),
            pltpu.VMEM((2, 8, 16, width), BF),
            pltpu.VMEM((2, 4, 2, 16, width), BF),
            DMA((3,)), DMA((DIRECT, 4)), DMA((DIRECT, 4)), DMA((2, 3, 4)), DMA((2, 3, 4)), DMA((1,)),
            DMA((5, 4)), DMA((5, 4)),
            DMA((8, 2)), DMA((8, 2)), DMA((8, 2)), DMA((8, 2)),
            DMA((2, 3, 4)), DMA((2, 3, 4)), DMA((len(HOME), 4)), DMA((len(HOME), 4)), DMA((5, 4)), DMA((5, 4)),
            DMA((2, 4, 2)), DMA((2, 4, 2)), DMA((2, 4, 2)), DMA((2, 4, 2)),
        ],
        compiler_params=pltpu.CompilerParams(
            collective_id=0, has_side_effects=True, vmem_limit_bytes=63 * 1024 * 1024
        ),
    )(sel, slot, tokens, cots, w, gate, up, down)


def shards(
    tokens,
    cotangent,
    dense_gate,
    dense_up,
    dense_down,
    expert_gate,
    expert_up,
    expert_down,
    expert_ids,
    route_weights,
):
    count, width = tokens.shape
    hid = dense_gate.shape[1]
    experts, cap = 16, 24
    y, x, c, z = place()

    flat_ids = expert_ids.reshape(-1)
    onehot = (flat_ids[:, None] == jnp.arange(experts, dtype=jnp.int32)[None, :]).astype(jnp.int32)
    earlier = jnp.cumsum(onehot, axis=0) - onehot
    placed = (flat_ids * cap + jnp.sum(earlier * onehot, axis=1)).reshape(count, 2)

    owner = (z + 8 + jnp.array(ORDER[:4], jnp.int32)) % 8
    y_d = jnp.arange(4, dtype=jnp.int32).reshape(2, 1, 2)
    x_d = (x + owner[None, :, None] // 2 + 2 * ((y_d + y) % 2)) % 4
    e_d = (y_d % 2) * 8 + x_d * 2 + ((c + owner) % 2)[None, :, None]
    row = jnp.arange(2 * cap, dtype=jnp.int32)
    slots = e_d[:, :, :, None] * cap + row % cap
    hits = slots[:, :, :, :, None, None] == placed
    weight = jnp.sum(jnp.where(hits, route_weights, 0.0), axis=(4, 5))
    slot = jnp.where(row < cap, 1.0, weight)[:, :, :, :, None]
    chosen = jnp.any(hits, axis=5)
    kind = (row < cap)[:, None]
    sel = jnp.concatenate([chosen & kind, chosen & ~kind], axis=4).astype(BF)

    dense_cat = jnp.concatenate([dense_gate, dense_up, dense_down.T], axis=1)
    input_grad, output, dense_grad, expert_grad = layer_call(
        sel, slot, tokens, cotangent, dense_cat, expert_gate[0].T, expert_up[0].T, expert_down[0]
    )
    return (
        output.reshape(count, width),
        input_grad.reshape(count, width),
        dense_grad[:, :hid],
        dense_grad[:, hid : 2 * hid],
        dense_grad[:, 2 * hid :].T,
        expert_grad[:hid].T[None],
        expert_grad[hid : 2 * hid].T[None],
        expert_grad[2 * hid :][None],
    )


def solution(mesh):
    in_specs = (
        P(("dp", "expert"), None),
        P(("dp", "expert"), None),
        P(("dp", "expert"), "tensor"),
        P(("dp", "expert"), "tensor"),
        P("tensor", ("dp", "expert")),
        P("expert", "dp", "tensor"),
        P("expert", "dp", "tensor"),
        P("expert", "tensor", "dp"),
        P(("dp", "expert"), None),
        P(("dp", "expert"), None),
    )
    out_specs = (
        P(("dp", "expert"), None),
        P(("dp", "expert"), None),
        P(("dp", "expert"), "tensor"),
        P(("dp", "expert"), "tensor"),
        P("tensor", ("dp", "expert")),
        P("expert", "dp", "tensor"),
        P("expert", "dp", "tensor"),
        P("expert", "tensor", "dp"),
    )
    return jax.shard_map(shards, mesh=mesh, in_specs=in_specs, out_specs=out_specs, check_vma=False)
```

time: 841 us -> 213 us (0.25)
  waiting for transfers between devices: 632 us -> 0 us
  Pallas kernels: 0 us -> 195 us
  matrix products: 54.6 us -> 0 us
  blocking collectives: 53.3 us -> 0 us
  local copies, waits for them, and re-layouts: 57.4 us -> 9.94 us
  starting transfers between devices: 21.7 us -> 0 us
  between operations: 14.2 us -> 0.84 us
    all_gather x6 -> x0, waiting for transfers between devices: 246 us -> none  [the longest x1 44.5 us: shards(): lax.all_gather(expert_gate[0], 'dp', axis=0, tiled=True)]
    reduce_scatter x7 -> x0, waiting for transfers between devices: 212 us -> none  [the longest x1 44.4 us: shards(): lax.psum_scatter(product(expert_hidden, weight_down).astype(jnp.bfloat16)...]
    pallas_call x0 -> x1, Pallas kernels: none -> 195 us  [layer_call(): pl.pallas_call(layer_kernel, out_shape=(shape((8, 16, width), BF), shape(...]
    unnamed x17 -> x0, waiting for transfers between devices: 140 us -> none
    dot_general x22 -> x0, matrix products: 54.6 us -> none  [the longest x8 21.2 us: product(): return jnp.dot(left, right, preferred_element_type=jnp.float32)]
    all_gather x2 -> x0, blocking collectives: 53.3 us -> none  [the longest x1 26.9 us: shards(): input_grad = lax.all_gather(grad_own, 'tensor', axis=1, tiled=True)]
    all_to_all x4 -> x0, waiting for transfers between devices: 34.3 us -> none  [the longest x1 34.3 us: shards(): lax.all_to_all(send_rows, 'expert', split_axis=0, concat_axis=0, tiled=True)]
    unnamed x45 -> x21, local copies, waits for them, and re-layouts: 39 us -> 5.24 us
  transfers between devices with their start and end apart: 19 -> 0, of which waited for: 15 -> 0; matrix products, arithmetic and copies ran while one was open for 13% -> 0% of each run, Pallas kernels for 0% -> 0%
where the time goes in v3:
time: 213 us; the launch traced here: 212 us
  Pallas kernels  195 us (92%)
  local copies, waits for them, and re-layouts  9.94 us (5%)
  other arithmetic  6.15 us (3%)
    pallas_call x1, Pallas kernels, layer_call(): pl.pallas_call(layer_kernel, out_shape=(shape((8, 16, width), BF), shape(...  195 us
    unnamed x21, local copies, waits for them, and re-layouts  5.24 us

profile of v3, /device:TPU:34, one launch (start us, length us, event | category | flops | bytes accessed | tf_op | source)
XLA Modules:
  0.0 212.3 jit_solution(12312002233078079073)
XLA Ops:
  0.7 0.7 fusion.16
  1.4 0.1 fusion.8
  1.5 0.1 broadcast_add_fusion
  1.6 0.8 copy.53
  2.4 0.1 eq.56
  2.5 0.6 reduce-window.6
  3.1 0.2 slice_reduce_fusion
  3.3 0.1 eq.52
  3.5 0.1 fusion.3
  3.6 0.1 reduce_sum.23
  3.7 0.1 copy.56
  3.8 0.7 multiply_add_fusion
  4.5 1.0 fusion
  5.5 0.0 copy-start.3
  5.5 0.0 copy-start.4
  5.5 0.2 copy.57
  5.7 0.0 copy-start.5
  5.8 0.8 broadcast_select_fusion.slot
  6.6 0.2 compare_reduce_fusion
  6.8 0.2 broadcast_and_fusion.1
  7.0 0.8 add_convert_fusion.sel
  7.8 0.0 copy-done.3
  7.8 0.1 copy.58
  7.9 0.0 copy-done.4
  7.9 0.1 copy.59
  8.0 0.0 copy-done.5
  8.1 0.1 copy.60
  8.2 0.8 pad_maximum_fusion.w
  9.0 195.4 %shard_map.170 = (bf16[8,16,3584]{2,1,0:T(8,128)(2,1)}, bf16[8,16,3584]{2,1,0:T(8,128)(2,1)}, bf16[112,912]{1,0:T(8,128)(2,1)}, bf16[912,1792]{1,0:T(8,128)(2,1)}) custom-call(bf16[2,4,2,48,256]{4,3,2,1,0:T(8,128)(2,1)} %add_convert_fusion.sel, f32[2,4,2,48,1]{4,3,2,1,0:T(8,128)} %broadcast_select_fusion.slot, bf16[128,3584]{1,0:T(8,128)(2,1)} %tokens.1, ...), custom_call_target="tpu_custom_call" | custom-call | tf_op jit(solution)/shard_map/pallas_call | solution.py:578
  204.4 0.0 copy-start.2
  204.4 3.7 %slice_bitcast_fusion = (bf16[1,304,1792]{2,1,0:T(8,128)(2,1)}, bf16[1,1792,304]{1,2,0:T(8,128)(2,1)}, bf16[1,1792,304]{1,2,0:T(8,128)(2,1)}) fusion(bf16[912,1792]{1,0:T(8,128)(2,1)} %get-tuple-element.15), kind=kLoop, calls=%fused_computation | loop fusion | bytes 6537216 | tf_op jit(solution)/shard_map/broadcast_in_dim | solution.py:665
  208.1 0.0 copy-start.1
  208.1 0.0 copy-done.2
  208.1 0.1 slice_bitcast_fusion.3
  208.2 0.7 copy.61
  209.0 0.0 copy-start
  209.0 0.7 copy.62
  209.7 0.7 copy.63
  210.5 0.0 copy-done.1
  210.5 0.9 copy.68
  211.4 0.0 copy-done
  211.4 0.9 copy.69
  (7 shorter events, 0.1 us)
Async XLA Ops:
  5.5 2.3 %copy-start.3 = (bf16[304,112]{1,0:T(8,128)(2,1)S(1)}, bf16[304,112]{1,0:T(8,128)(2,1)}, u32[]{:S(2)}) copy-start(bf16[304,112]{1,0:T(8,128)(2,1)} %param.15) | copy-start | bytes 204292
  5.5 2.4 %copy-start.4 = (bf16[112,304]{0,1:T(8,128)(2,1)S(1)}, bf16[112,304]{0,1:T(8,128)(2,1)}, u32[]{:S(2)}) copy-start(bf16[112,304]{0,1:T(8,128)(2,1)} %param.13) | copy-start | bytes 204292
  5.7 2.3 %copy-start.5 = (bf16[112,304]{0,1:T(8,128)(2,1)S(1)}, bf16[112,304]{0,1:T(8,128)(2,1)}, u32[]{:S(2)}) copy-start(bf16[112,304]{0,1:T(8,128)(2,1)} %param.14) | copy-start | bytes 204292
  204.4 3.7 %copy-start.2 = (bf16[112,912]{1,0:T(8,128)(2,1)S(1)}, bf16[112,912]{1,0:T(8,128)(2,1)}, u32[]{:S(2)}) copy-start(bf16[112,912]{1,0:T(8,128)(2,1)} %get-tuple-element.14) | copy-start | bytes 612868
  208.1 2.4 %copy-start.1 = (bf16[8,16,3584]{2,1,0:T(8,128)(2,1)S(1)}, bf16[8,16,3584]{2,1,0:T(8,128)(2,1)}, u32[]{:S(2)}) copy-start(bf16[8,16,3584]{2,1,0:T(8,128)(2,1)} %get-tuple-element.12) | copy-start | bytes 2752516
  209.0 2.4 %copy-start = (bf16[8,16,3584]{2,1,0:T(8,128)(2,1)S(1)}, bf16[8,16,3584]{2,1,0:T(8,128)(2,1)}, u32[]{:S(2)}) copy-start(bf16[8,16,3584]{2,1,0:T(8,128)(2,1)} %get-tuple-element.13) | copy-start | bytes 2752516

commit v4 on v3

--- a/solution.py
+++ b/solution.py
@@ -88,7 +88,7 @@
 
 def layer_kernel(
     sel, slot, tokens, cots, w, gate, up, down,
-    back, out, dgrad, wgrad,
+    back, out, dgrad, ggrad, ugrad, lgrad,
     send, wt, recv, full, cr, mine, theirs, via, acts, spread, part, rr, ra, rb, rc, rd, ret, tot, rz,
     wt_s, dsp_s, dsp_r, ag_s, ag_r, loc, da_s, da_r, near_s, near_r, far_s, far_r,
     ring_s, ring_r, ret_s, ret_r, d_s, d_r, rs_s, rs_r, fin_s, fin_r,
@@ -176,6 +176,8 @@
         disp(0, j, "start")
     for r in range(1, DIRECT):
         build(r)
+        for j in range(4):
+            disp(r, j, "start")
 
 
     own = pltpu.make_async_copy(w, full.at[y, x, c], loc.at[0])
@@ -394,9 +396,14 @@
         dgrad[...] = cr[y, x]
 
 
-    def expert_weights(first, count):
-        rows = acts[:, :, :, first : first + count].reshape(1536, count)
-        wgrad[first : first + count, :] = transposed_times(rows, recv[...].reshape(1536, half)).astype(BF)
+    def expert_weights(i):
+        first, last = 256 * i, min(256 * (i + 1), 3 * hid)
+        rows = acts[:, :, :, first:last].reshape(1536, last - first)
+        value = transposed_times(rows, recv[...].reshape(1536, half)).astype(BF)
+        for q, ref in enumerate((ggrad, ugrad, lgrad)):
+            low, high = max(first, q * hid), min(last, (q + 1) * hid)
+            if low < high:
+                ref[low - q * hid : high - q * hid, :] = value[low - first : high - first]
 
 
     outs = (back, out)
@@ -433,9 +440,6 @@
         disp(0, j, "wait_recv")
         carry(0, 1, j).start()
         carry(1, 1, j).start()
-    for r in range(1, DIRECT):
-        for j in range(4):
-            disp(r, j, "start")
     for copy in ga:
         copy.start()
     for copy in weights:
@@ -450,8 +454,6 @@
     relay(0)
     pre_block(4)
     pre_block(5)
-    own.wait()
-    after(gb, gc)
     relay(1)
     relay(2)
     carry_step(3)
@@ -463,44 +465,42 @@
     pre_block(7)
     relay(4)
     relay(5)
-    after(gc, gd)
     relay(6)
     relay(7)
     for direction in (0, 1):
         for j in carried(direction, 3):
             carry(direction, 3, j).wait_recv()
     pre_block(3)
+    own.wait()
+    after(gb, gc)
     results_block(6)
     results_block(7)
+    ring_step(2)
     relay(3)
-    ring_step(2)
-    after(gd, ge)
+    results_block(4)
+    results_block(5)
     results_block(3)
     for j in range(4):
         home(3, j, "start")
-    results_block(4)
-    results_block(5)
-    after(ge, ())
-    dense_forward()
     ring_step(3)
+    after(gc, gd)
     results_block(0)
-    for copy in ga + gb + gc + gd + ge:
-        copy.wait_send()
-    dense_weights()
-    for copy in s_one:
-        copy.start()
+    expert_weights(0)
+    expert_weights(1)
+    after(gd, ge)
     for k in range(4):
         hop(0, 3, k).wait_recv()
         hop(1, 3, k).wait_recv()
         add_into(rr.at[0, 2, k], rr.at[1, 2, k], part.at[z, k])
     for j in range(4):
         home(0, j, "start")
-    scatter_two()
-    expert_weights(0, 256)
-    scatter_three()
-    for i in range(1, 3):
-        expert_weights(256 * i, 256)
-    expert_weights(768, 3 * hid - 768)
+    after(ge, ())
+    dense_forward()
+    for copy in ga + gb + gc + gd + ge:
+        copy.wait_send()
+    dense_weights()
+    for copy in s_one:
+        copy.start()
     for r in HOME:
         for j in range(4):
             home(r, j, "wait_recv")
@@ -516,12 +516,15 @@
         final_hop(direction, 1, direction).start()
     for direction in (0, 1):
         final_hop(direction, 2, 1 - direction).start()
+    expert_weights(2)
+    scatter_two()
+    final_step(2)
+    expert_weights(3)
+    scatter_three()
+    final_step(3)
     scatter_four()
-    final_step(2)
+    final_step(4)
     scatter_five()
-    final_step(3)
-    final_step(4)
-    scatter_end()
     mine_rows = pl.ds(pl.multiple_of(z * 16, 16), 16)
     for q in (0, 1):
         final_hop(0, 4, q).wait_recv()
@@ -539,6 +542,7 @@
                     share(direction, t, q).start()
     for direction in (0, 1):
         share(direction, 4, direction).wait_recv()
+    scatter_end()
 
 
     for r in range(DIRECT):
@@ -581,10 +585,12 @@
             shape((8, 16, width), BF),
             shape((8, 16, width), BF),
             shape((112, lanes), BF),
-            shape((lanes, half), BF),
+            shape((hid, half), BF),
+            shape((hid, half), BF),
+            shape((hid, half), BF),
         ),
         in_specs=[VMEM] * 4 + [HBM] * 4,
-        out_specs=(VMEM,) * 4,
+        out_specs=(VMEM,) * 6,
         scratch_shapes=[
             pltpu.VMEM((2, DIRECT, 2, 48, half), BF),
             pltpu.VMEM((lanes, half), BF),
@@ -651,7 +657,7 @@
     sel = jnp.concatenate([chosen & kind, chosen & ~kind], axis=4).astype(BF)
 
     dense_cat = jnp.concatenate([dense_gate, dense_up, dense_down.T], axis=1)
-    input_grad, output, dense_grad, expert_grad = layer_call(
+    input_grad, output, dense_grad, gate_grad, up_grad, down_grad = layer_call(
         sel, slot, tokens, cotangent, dense_cat, expert_gate[0].T, expert_up[0].T, expert_down[0]
     )
     return (
@@ -660,9 +666,9 @@
         dense_grad[:, :hid],
         dense_grad[:, hid : 2 * hid],
         dense_grad[:, 2 * hid :].T,
-        expert_grad[:hid].T[None],
-        expert_grad[hid : 2 * hid].T[None],
-        expert_grad[2 * hid :][None],
+        gate_grad.T[None],
+        up_grad.T[None],
+        down_grad[None],
     )
 
 

time: 213 us -> 202 us (0.948)
  Pallas kernels: 195 us -> 181 us
  local copies, waits for them, and re-layouts: 9.94 us -> 12.2 us
    pallas_call x1, Pallas kernels: 195 us -> 181 us  [layer_call(): pl.pallas_call(layer_kernel, out_shape=(shape((8, 16, width), BF), shape(...]
    unnamed x21 -> x28, local copies, waits for them, and re-layouts: 5.24 us -> 10.1 us
    broadcast_in_dim x1 -> x0, local copies, waits for them, and re-layouts: 3.71 us -> none  [shards(): expert_grad[2 * hid:][None]]
where the time goes in v4:
time: 202 us; the launch traced here: 201 us
  Pallas kernels  181 us (90%)
  local copies, waits for them, and re-layouts  12.2 us (6%)
  other arithmetic  6.15 us (3%)
    pallas_call x1, Pallas kernels, layer_call(): pl.pallas_call(layer_kernel, out_shape=(shape((8, 16, width), BF), shape(...  181 us
    unnamed x28, local copies, waits for them, and re-layouts  10.1 us

profile of v4, /device:TPU:34, one launch (start us, length us, event | category | flops | bytes accessed | tf_op | source)
XLA Modules:
  0.0 200.6 jit_solution(6597948626768081518)
XLA Ops:
  0.7 0.7 fusion.16
  1.4 0.1 fusion.8
  1.5 0.1 broadcast_add_fusion
  1.6 0.8 copy.53
  2.4 0.1 eq.56
  2.5 0.6 reduce-window.6
  3.1 0.2 slice_reduce_fusion
  3.3 0.1 eq.52
  3.5 0.1 fusion.3
  3.6 0.1 reduce_sum.23
  3.7 0.1 copy.56
  3.8 0.7 multiply_add_fusion
  4.5 1.0 fusion
  5.5 0.0 copy-start.5
  5.5 0.0 copy-start.6
  5.5 0.2 copy.57
  5.7 0.0 copy-start.7
  5.8 0.8 broadcast_select_fusion.slot
  6.6 0.2 compare_reduce_fusion
  6.8 0.2 broadcast_and_fusion.1
  7.0 0.8 add_convert_fusion.sel
  7.8 0.0 copy-done.5
  7.8 0.1 copy.58
  7.9 0.0 copy-done.6
  7.9 0.1 copy.59
  8.0 0.0 copy-done.7
  8.1 0.1 copy.60
  8.2 0.8 pad_maximum_fusion.w
  9.0 181.4 %shard_map.170 = (bf16[8,16,3584]{2,1,0:T(8,128)(2,1)}, bf16[8,16,3584]{2,1,0:T(8,128)(2,1)}, bf16[112,912]{1,0:T(8,128)(2,1)}, bf16[304,1792]{1,0:T(8,128)(2,1)...) custom-call(bf16[2,4,2,48,256]{4,3,2,1,0:T(8,128)(2,1)} %add_convert_fusion.sel, ...), custom_call_target="tpu_custom_call" | custom-call | tf_op jit(solution)/shard_map/pallas_call | solution.py:582
  190.4 0.0 copy-start.4
  190.4 1.2 slice_bitcast_fusion
  191.6 0.7 copy.61
  192.3 0.0 copy-start.3
  192.3 0.7 copy.62
  193.1 0.7 copy.63
  193.8 0.0 copy-done.4
  193.8 0.9 copy.71
  194.8 0.0 copy-done.3
  194.8 0.0 copy-start.2
  194.8 0.9 copy.72
  195.7 0.6 copy-done.2
  196.3 0.0 copy-start.1
  196.3 1.0 copy.73
  197.3 0.6 copy-done.1
  198.0 0.0 copy-start
  198.0 1.0 copy.74
  198.9 0.6 copy-done
  199.6 1.0 copy.75
  (7 shorter events, 0.1 us)
Async XLA Ops:
  5.5 2.3 %copy-start.5 = (bf16[304,112]{1,0:T(8,128)(2,1)S(1)}, bf16[304,112]{1,0:T(8,128)(2,1)}, u32[]{:S(2)}) copy-start(bf16[304,112]{1,0:T(8,128)(2,1)} %param.15) | copy-start | bytes 204292
  5.5 2.4 %copy-start.6 = (bf16[112,304]{0,1:T(8,128)(2,1)S(1)}, bf16[112,304]{0,1:T(8,128)(2,1)}, u32[]{:S(2)}) copy-start(bf16[112,304]{0,1:T(8,128)(2,1)} %param.13) | copy-start | bytes 204292
  5.7 2.3 %copy-start.7 = (bf16[112,304]{0,1:T(8,128)(2,1)S(1)}, bf16[112,304]{0,1:T(8,128)(2,1)}, u32[]{:S(2)}) copy-start(bf16[112,304]{0,1:T(8,128)(2,1)} %param.14) | copy-start | bytes 204292
  190.4 3.4 %copy-start.4 = (bf16[8,16,3584]{2,1,0:T(8,128)(2,1)S(1)}, bf16[8,16,3584]{2,1,0:T(8,128)(2,1)}, u32[]{:S(2)}) copy-start(bf16[8,16,3584]{2,1,0:T(8,128)(2,1)} %get-tuple-element.14) | copy-start | bytes 2752516
  192.3 2.4 %copy-start.3 = (bf16[8,16,3584]{2,1,0:T(8,128)(2,1)S(1)}, bf16[8,16,3584]{2,1,0:T(8,128)(2,1)}, u32[]{:S(2)}) copy-start(bf16[8,16,3584]{2,1,0:T(8,128)(2,1)} %get-tuple-element.15) | copy-start | bytes 2752516
  194.8 1.6 copy-start.2
  196.3 1.6 copy-start.1
  198.0 1.6 copy-start

commit v5 on v4

--- a/solution.py
+++ b/solution.py
@@ -520,11 +520,9 @@
     scatter_two()
     final_step(2)
     expert_weights(3)
+    final_step(3)
     scatter_three()
-    final_step(3)
-    scatter_four()
     final_step(4)
-    scatter_five()
     mine_rows = pl.ds(pl.multiple_of(z * 16, 16), 16)
     for q in (0, 1):
         final_hop(0, 4, q).wait_recv()
@@ -534,12 +532,15 @@
         outs[q][z] = total.astype(BF)
         for direction in (0, 1):
             share(direction, 1, q).start()
+    scatter_four()
     for t in (2, 3, 4):
         for q in (0, 1):
             for direction in (0, 1):
                 share(direction, t - 1, q).wait_recv()
                 if t < 4 or q == direction:
                     share(direction, t, q).start()
+        if t == 2:
+            scatter_five()
     for direction in (0, 1):
         share(direction, 4, direction).wait_recv()
     scatter_end()

time: 202 us -> 192 us (0.950)
  Pallas kernels: 181 us -> 169 us
    pallas_call x1, Pallas kernels: 181 us -> 169 us  [layer_call(): pl.pallas_call(layer_kernel, out_shape=(shape((8, 16, width), BF), shape(...]
where the time goes in v5:
time: 192 us; the launch traced here: 189 us
  Pallas kernels  169 us (88%)
  local copies, waits for them, and re-layouts  12.2 us (6%)
  other arithmetic  6.15 us (3%)
    pallas_call x1, Pallas kernels, layer_call(): pl.pallas_call(layer_kernel, out_shape=(shape((8, 16, width), BF), shape(...  169 us
    unnamed x28, local copies, waits for them, and re-layouts  10.1 us

profile of v5, /device:TPU:34, one launch (start us, length us, event | category | flops | bytes accessed | tf_op | source)
XLA Modules:
  0.0 188.6 jit_solution(809561947328230532)
XLA Ops:
  0.7 0.7 fusion.16
  1.4 0.1 fusion.8
  1.5 0.1 broadcast_add_fusion
  1.6 0.8 copy.53
  2.4 0.1 eq.56
  2.5 0.6 reduce-window.6
  3.1 0.2 slice_reduce_fusion
  3.3 0.1 eq.52
  3.5 0.1 fusion.3
  3.6 0.1 reduce_sum.23
  3.7 0.1 copy.56
  3.8 0.7 multiply_add_fusion
  4.5 1.0 fusion
  5.5 0.0 copy-start.5
  5.5 0.0 copy-start.6
  5.5 0.2 copy.57
  5.7 0.0 copy-start.7
  5.8 0.8 broadcast_select_fusion.slot
  6.6 0.2 compare_reduce_fusion
  6.8 0.2 broadcast_and_fusion.1
  7.0 0.8 add_convert_fusion.sel
  7.8 0.0 copy-done.5
  7.8 0.1 copy.58
  7.9 0.0 copy-done.6
  7.9 0.1 copy.59
  8.0 0.0 copy-done.7
  8.1 0.1 copy.60
  8.2 0.8 pad_maximum_fusion.w
  9.0 169.4 %shard_map.170 = (bf16[8,16,3584]{2,1,0:T(8,128)(2,1)}, bf16[8,16,3584]{2,1,0:T(8,128)(2,1)}, bf16[112,912]{1,0:T(8,128)(2,1)}, bf16[304,1792]{1,0:T(8,128)(2,1)...) custom-call(bf16[2,4,2,48,256]{4,3,2,1,0:T(8,128)(2,1)} %add_convert_fusion.sel, ...), custom_call_target="tpu_custom_call" | custom-call | tf_op jit(solution)/shard_map/pallas_call | solution.py:583
  178.5 0.0 copy-start.4
  178.5 1.2 slice_bitcast_fusion
  179.7 0.7 copy.61
  180.4 0.0 copy-start.3
  180.4 0.7 copy.62
  181.2 0.7 copy.63
  181.9 0.0 copy-done.4
  181.9 0.9 copy.71
  182.8 0.0 copy-done.3
  182.8 0.0 copy-start.2
  182.8 0.9 copy.72
  183.8 0.6 copy-done.2
  184.4 0.0 copy-start.1
  184.4 1.0 copy.73
  185.4 0.6 copy-done.1
  186.0 0.0 copy-start
  186.0 1.0 copy.74
  187.0 0.6 copy-done
  187.7 1.0 copy.75
  (7 shorter events, 0.1 us)
Async XLA Ops:
  5.5 2.3 %copy-start.5 = (bf16[304,112]{1,0:T(8,128)(2,1)S(1)}, bf16[304,112]{1,0:T(8,128)(2,1)}, u32[]{:S(2)}) copy-start(bf16[304,112]{1,0:T(8,128)(2,1)} %param.15) | copy-start | bytes 204292
  5.5 2.4 %copy-start.6 = (bf16[112,304]{0,1:T(8,128)(2,1)S(1)}, bf16[112,304]{0,1:T(8,128)(2,1)}, u32[]{:S(2)}) copy-start(bf16[112,304]{0,1:T(8,128)(2,1)} %param.13) | copy-start | bytes 204292
  5.7 2.3 %copy-start.7 = (bf16[112,304]{0,1:T(8,128)(2,1)S(1)}, bf16[112,304]{0,1:T(8,128)(2,1)}, u32[]{:S(2)}) copy-start(bf16[112,304]{0,1:T(8,128)(2,1)} %param.14) | copy-start | bytes 204292
  178.5 3.4 %copy-start.4 = (bf16[8,16,3584]{2,1,0:T(8,128)(2,1)S(1)}, bf16[8,16,3584]{2,1,0:T(8,128)(2,1)}, u32[]{:S(2)}) copy-start(bf16[8,16,3584]{2,1,0:T(8,128)(2,1)} %get-tuple-element.14) | copy-start | bytes 2752516
  180.4 2.4 %copy-start.3 = (bf16[8,16,3584]{2,1,0:T(8,128)(2,1)S(1)}, bf16[8,16,3584]{2,1,0:T(8,128)(2,1)}, u32[]{:S(2)}) copy-start(bf16[8,16,3584]{2,1,0:T(8,128)(2,1)} %get-tuple-element.15) | copy-start | bytes 2752516
  182.8 1.6 copy-start.2
  184.4 1.6 copy-start.1
  186.0 1.6 copy-start
